TPU v7x, 128 devices: a whole 4x4x4 slice. The times are simulated.
128 devices in a mesh: gy: 8 (over z_lo, y), gx: 16 (over z_hi, x, core).
Axes of the slice: x: 4, y: 4, z: 4 (z_hi: 2, z_lo: 2; z = z_hi * 2 + z_lo), core: 2. Of those that a mesh axis runs over, the one named last changes fastest.
Arguments:
- occupancy: int32 [2, 40, 512, 512], P(None, None, 'gy', 'gx'), may hold values 0 or 1
- counts: int32 [2, 512, 512], P(None, 'gy', 'gx'), may hold values from 0 to 64
- level_embed: bfloat16 [40, 256], replicated, may hold values from -1.796875 to 1.796875
- count_weight: float32 [256], replicated, may hold values from -3 to 3
- norm_gains: float32 [2, 256], replicated, may hold values from 0.1 to 1.9
- row_qkv: bfloat16 [256, 768], replicated, may hold values from -2 to 2
- row_out: bfloat16 [256, 256], replicated, may hold values from -0.375 to 0.375
- col_qkv: bfloat16 [256, 768], replicated, may hold values from -2 to 2
- col_out: bfloat16 [256, 256], replicated, may hold values from -0.375 to 0.375
- depth_kernel: float32 [3, 3, 256], replicated, may hold values from -2 to 2
- point_weight: bfloat16 [256, 256], replicated, may hold values from -0.375 to 0.375
Outputs:
- bev_out: bfloat16 [2, 512, 512, 256], P(None, 'gy', 'gx')
All inputs are finite; a program needn't handle non-finite values. No bound on the sum of `occupancy` on one device may be relied on, other than what follows from the above.
Results may differ from a plain program's by a relative error of at most 0.015.
The roundings to bfloat16 on the way count: a program that leaves them out, or rounds other values in their place, can miss the bound.
Values may be sent and summed in bfloat16 or wider, within the bound.
A program may use at most 128 MiB of HBM per device.

v0:
```python
import jax
import jax.numpy as jnp
from jax import lax
from jax.sharding import PartitionSpec as P

HEADS = 8


def extended(array, sides, width):
    for axis, dim in sides:
        size, length = (lax.axis_size(axis), array.shape[dim])
        up = [(i, (i + 1) % size) for i in range(size - 1)]
        down = [(j, i) for i, j in up]
        last = lax.slice_in_dim(array, length - width, length, axis=dim)
        first = lax.slice_in_dim(array, 0, width, axis=dim)
        before = lax.ppermute(last, axis, up)
        after = lax.ppermute(first, axis, down)
        array = jnp.concatenate([before, array, after], axis=dim)
    return array


def layer_norm(source, gain_vec):
    wide_x = source.astype(jnp.float32)
    row_mean = jnp.mean(wide_x, -1, keepdims=True)
    centred = wide_x - row_mean
    variance = jnp.mean(centred * centred, -1, keepdims=True)
    return (centred * lax.rsqrt(variance + 1e-05) * gain_vec).astype(jnp.bfloat16)


def attend_line(packed):
    channels = packed.shape[-1] // 3
    length = packed.shape[0]
    head_dim = channels // HEADS
    queries = packed[:, :channels].reshape(length, HEADS, head_dim)
    keyset = packed[:, channels : 2 * channels].reshape(length, HEADS, head_dim)
    values = packed[:, 2 * channels :].reshape(length, HEADS, head_dim)
    scores = jnp.einsum(
        "qhd,khd->hqk", queries, keyset, preferred_element_type=jnp.float32
    ) * head_dim ** (-0.5)
    row_max = jnp.max(scores, -1, keepdims=True)
    weights = jnp.exp(scores - row_max)
    probs = (weights / jnp.sum(weights, -1, keepdims=True)).astype(jnp.bfloat16)
    attended = jnp.einsum("hqk,khd->qhd", probs, values, preferred_element_type=jnp.float32)
    return attended.reshape(length, channels).astype(jnp.bfloat16)


def axial(source, gain_vec, w_qkv, w_out, line_dim):
    normed = layer_norm(source, gain_vec)
    packed = jnp.dot(normed, w_qkv, preferred_element_type=jnp.float32).astype(jnp.bfloat16)
    if line_dim == 1:
        packed = packed.transpose(0, 2, 1, 3)
    dims_now = packed.shape
    per_turn = max(1, 1024 // dims_now[2])
    attended = lax.map(
        attend_line, packed.reshape(-1, dims_now[2], dims_now[3]), batch_size=per_turn
    )
    attended = attended.reshape(dims_now[0], dims_now[1], dims_now[2], -1)
    if line_dim == 1:
        attended = attended.transpose(0, 2, 1, 3)
    return (
        source.astype(jnp.float32) + jnp.dot(attended, w_out, preferred_element_type=jnp.float32)
    ).astype(jnp.bfloat16)


def per_device(
    occupancy,
    counts,
    level_embed,
    count_weight,
    norm_gains,
    row_qkv,
    row_out,
    col_qkv,
    col_out,
    depth_kernel,
    point_weight,
):
    base = jnp.einsum(
        "blhw,lc->bhwc",
        occupancy.astype(jnp.bfloat16),
        level_embed,
        preferred_element_type=jnp.float32,
    )
    count_term = jnp.log1p(counts.astype(jnp.float32))[..., None] * count_weight
    pillars = (base + count_term).astype(jnp.bfloat16)
    rows_done = axial(
        lax.all_to_all(pillars, "gx", split_axis=1, concat_axis=2, tiled=True),
        norm_gains[0],
        row_qkv,
        row_out,
        2,
    )
    tiles = lax.all_to_all(rows_done, "gx", split_axis=2, concat_axis=1, tiled=True)
    columns = lax.all_to_all(tiles, "gy", split_axis=2, concat_axis=1, tiled=True)
    col_section = axial(columns, norm_gains[1], col_qkv, col_out, 1)
    cols_done = lax.all_to_all(col_section, "gy", split_axis=1, concat_axis=2, tiled=True)
    tile_rows = cols_done.shape[1]
    tile_cols = cols_done.shape[2]
    padded = extended(cols_done, (("gy", 1), ("gx", 2)), 1)
    depth_sum = jnp.zeros(cols_done.shape, jnp.float32)
    for row_off in range(3):
        for col_off in range(3):
            depth_sum = (
                depth_sum
                + padded[:, row_off : row_off + tile_rows, col_off : col_off + tile_cols, :].astype(
                    jnp.float32
                )
                * depth_kernel[row_off, col_off]
            )
    activated = jax.nn.silu(depth_sum).astype(jnp.bfloat16)
    return (
        cols_done.astype(jnp.float32)
        + jnp.dot(activated, point_weight, preferred_element_type=jnp.float32)
    ).astype(jnp.bfloat16)


def solution(mesh):
    in_specs = (
        P(None, None, "gy", "gx"),
        P(None, "gy", "gx"),
        P(),
        P(),
        P(),
        P(),
        P(),
        P(),
        P(),
        P(),
        P(),
    )
    out_specs = P(None, "gy", "gx", None)
    return jax.shard_map(
        per_device, mesh=mesh, in_specs=in_specs, out_specs=out_specs, check_vma=False
    )
```

profile of v0, /device:TPU:1, one launch (start us, length us, event | category | flops | bytes accessed | tf_op | source)
XLA Modules:
  0.0 371.9 jit_solution(3110964276050615189)
XLA Ops:
  7.5 9.1 %all-to-all-start = ((bf16[2,64,32,256]{3,2,0,1:T(8,128)(2,1)}), bf16[2,64,32,256]{3,2,0,1:T(8,128)(2,1)S(1)}, u32[]{:S(2)}, u32[]{:S(2)}) async-start(bf16[2,64,32,256]{3,2,0,1:T(8,128)(2,1)} %copy.102), calls=%async_computation | async-start | bytes 4194304 | tf_op jit(solution)/shard_map/all_to_all | solution.py:87
  17.1 28.1 %all-to-all-done = bf16[2,64,32,256]{3,2,0,1:T(8,128)(2,1)S(1)} async-done(((bf16[2,64,32,256]{3,2,0,1:T(8,128)(2,1)}), bf16[2,64,32,256]{3,2,0,1:T(8,128)(2,1)S(1)}, u32[]{:S(2)}, u32[]{:S(2)}) %all-to-all-start) | async-done | bytes 2097184 | tf_op jit(solution)/shard_map/all_to_all | solution.py:87
  51.8 4.4 %convolution_convert_fusion.1 = bf16[2,4,512,768]{3,2,1,0:T(8,128)(2,1)} fusion(bf16[2,4,512,256]{3,2,1,0:T(8,128)(2,1)S(1)} %fusion.32, bf16[256,768]{1,0:T(8,128)(2,1)S(1)} %copy-done), kind=kOutput, calls=%fused_computation.57 | convolution fusion | flops 1613758464 | bytes 8781824 | tf_op jit(solution)/shard_map/dot_general | solution.py:49
  57.8 77.6 %while.20 = (s32[]{:T(128)}, bf16[4,2,512,256]{2,3,1,0:T(8,128)(2,1)}, bf16[4,2,512,768]{3,2,1,0:T(8,128)(2,1)}, s32[]{:T(128)}) while((s32[]{:T(128)}, bf16[4,2,512,256]{2,3,1,0:T(8,128)(2,1)}, bf16[4,2,512,768]{3,2,1,0:T(8,128)(2,1)}, s32[]{:T(128)}) %tuple.75), condition=%wide.region_5.6_spmd, body=%wide.region_2.5_spmd.sunk | while | flops 558105088 | bytes 46203448 | solution.py:54
  60.2 8.8 %fusion.107 = (f32[2,8,512]{2,1,0:T(8,128)S(1)}, f32[2,8,512,512]{2,3,1,0:T(8,128)}) fusion(bf16[2,512,8,32]{1,3,2,0:T(8,128)(2,1)S(1)} %bitcast.187, bf16[2,512,8,32]{1,3,2,0:T(8,128)(2,1)S(1)} %bitcast.186), kind=kOutput, calls=%fused_computation.107.clone.1 | convolution fusion | flops 281018880 | bytes 17858560 | tf_op jit(solution)/shard_map/while/body/eval_jaxpr/vmap()/sub | solution.py:41
  69.0 7.3 %fusion.108 = bf16[2,8,32,512]{3,2,1,0:T(8,128)(2,1)S(1)} fusion(bf16[2,512,8,32]{1,3,2,0:T(8,128)(2,1)S(1)} %bitcast.184, f32[2,8,512,512]{2,3,1,0:T(8,128)} %get-tuple-element.162, f32[2,8,512]{2,1,0:T(8,128)S(1)} %get-tuple-element.163), kind=kOutput, calls=%fused_computation.8.clone.1 | convolution fusion | flops 277086208 | bytes 17858560 | tf_op jit(solution)/shard_map/while/body/eval_jaxpr/vmap(hqk,khd->qhd)/dot_general | solution.py:43
  79.6 8.8 %fusion.107 = (f32[2,8,512]{2,1,0:T(8,128)S(1)}, f32[2,8,512,512]{2,3,1,0:T(8,128)}) fusion(bf16[2,512,8,32]{1,3,2,0:T(8,128)(2,1)S(1)} %bitcast.187, bf16[2,512,8,32]{1,3,2,0:T(8,128)(2,1)S(1)} %bitcast.186), kind=kOutput, calls=%fused_computation.107.clone.1 | convolution fusion | flops 281018880 | bytes 17858560 | tf_op jit(solution)/shard_map/while/body/eval_jaxpr/vmap()/sub | solution.py:41
  88.4 7.3 %fusion.108 = bf16[2,8,32,512]{3,2,1,0:T(8,128)(2,1)S(1)} fusion(bf16[2,512,8,32]{1,3,2,0:T(8,128)(2,1)S(1)} %bitcast.184, f32[2,8,512,512]{2,3,1,0:T(8,128)} %get-tuple-element.162, f32[2,8,512]{2,1,0:T(8,128)S(1)} %get-tuple-element.163), kind=kOutput, calls=%fused_computation.8.clone.1 | convolution fusion | flops 277086208 | bytes 17858560 | tf_op jit(solution)/shard_map/while/body/eval_jaxpr/vmap(hqk,khd->qhd)/dot_general | solution.py:43
  99.0 8.8 %fusion.107 = (f32[2,8,512]{2,1,0:T(8,128)S(1)}, f32[2,8,512,512]{2,3,1,0:T(8,128)}) fusion(bf16[2,512,8,32]{1,3,2,0:T(8,128)(2,1)S(1)} %bitcast.187, bf16[2,512,8,32]{1,3,2,0:T(8,128)(2,1)S(1)} %bitcast.186), kind=kOutput, calls=%fused_computation.107.clone.1 | convolution fusion | flops 281018880 | bytes 17858560 | tf_op jit(solution)/shard_map/while/body/eval_jaxpr/vmap()/sub | solution.py:41
  107.8 7.3 %fusion.108 = bf16[2,8,32,512]{3,2,1,0:T(8,128)(2,1)S(1)} fusion(bf16[2,512,8,32]{1,3,2,0:T(8,128)(2,1)S(1)} %bitcast.184, f32[2,8,512,512]{2,3,1,0:T(8,128)} %get-tuple-element.162, f32[2,8,512]{2,1,0:T(8,128)S(1)} %get-tuple-element.163), kind=kOutput, calls=%fused_computation.8.clone.1 | convolution fusion | flops 277086208 | bytes 17858560 | tf_op jit(solution)/shard_map/while/body/eval_jaxpr/vmap(hqk,khd->qhd)/dot_general | solution.py:43
  118.4 8.8 %fusion.107 = (f32[2,8,512]{2,1,0:T(8,128)S(1)}, f32[2,8,512,512]{2,3,1,0:T(8,128)}) fusion(bf16[2,512,8,32]{1,3,2,0:T(8,128)(2,1)S(1)} %bitcast.187, bf16[2,512,8,32]{1,3,2,0:T(8,128)(2,1)S(1)} %bitcast.186), kind=kOutput, calls=%fused_computation.107.clone.1 | convolution fusion | flops 281018880 | bytes 17858560 | tf_op jit(solution)/shard_map/while/body/eval_jaxpr/vmap()/sub | solution.py:41
  127.2 7.3 %fusion.108 = bf16[2,8,32,512]{3,2,1,0:T(8,128)(2,1)S(1)} fusion(bf16[2,512,8,32]{1,3,2,0:T(8,128)(2,1)S(1)} %bitcast.184, f32[2,8,512,512]{2,3,1,0:T(8,128)} %get-tuple-element.162, f32[2,8,512]{2,1,0:T(8,128)S(1)} %get-tuple-element.163), kind=kOutput, calls=%fused_computation.8.clone.1 | convolution fusion | flops 277086208 | bytes 17858560 | tf_op jit(solution)/shard_map/while/body/eval_jaxpr/vmap(hqk,khd->qhd)/dot_general | solution.py:43
  135.3 3.8 %fusion.33 = bf16[2,4,512,256]{3,2,1,0:T(8,128)(2,1)S(1)} fusion(f32[2,16,4,32,256]{4,3,1,2,0:T(8,128)} %copy-done.3, bf16[256,256]{1,0:T(8,128)(2,1)S(1)} %copy-done.5, bf16[2,4,512,256]{2,3,1,0:T(8,128)(2,1)} %bitcast.141), kind=kOutput, calls=%fused_computation.44 | convolution fusion | flops 538968064 | bytes 8519680 | tf_op jit(solution)/shard_map/dot_general | solution.py:61
  140.7 33.5 %all_to_all.54 = bf16[2,4,512,256]{3,1,0,2:T(4,128)(2,1)S(1)} all-to-all(bf16[2,4,512,256]{3,1,0,2:T(4,128)(2,1)S(1)} %copy.106), channel_id=1, replica_groups=mesh['gy'=8,'gx'=16] {'gx'}, dimensions={2} | all-to-all | bytes 4194304 | tf_op jit(solution)/shard_map/all_to_all | solution.py:93
  176.1 30.1 %all_to_all.55 = bf16[2,64,32,256]{3,1,0,2:T(8,128)(2,1)S(1)} all-to-all(bf16[2,64,32,256]{3,1,0,2:T(8,128)(2,1)S(1)} %copy.109), channel_id=1, replica_groups=mesh['gy'=8,'gx'=16] {'gy'}, dimensions={2} | all-to-all | bytes 4194304 | tf_op jit(solution)/shard_map/all_to_all | solution.py:94
  217.0 4.4 %convolution_convert_fusion = bf16[2,512,4,768]{3,1,2,0:T(8,128)(2,1)} fusion(bf16[2,512,4,256]{3,1,2,0:T(8,128)(2,1)S(1)} %fusion.28, bf16[256,768]{1,0:T(8,128)(2,1)S(1)} %copy-done.4), kind=kOutput, calls=%fused_computation.56 | convolution fusion | flops 1613758464 | bytes 8781824 | tf_op jit(solution)/shard_map/dot_general | solution.py:49
  222.9 77.5 %while.21 = (s32[]{:T(128)}, bf16[4,2,512,256]{2,3,1,0:T(8,128)(2,1)}, bf16[4,2,512,768]{3,2,1,0:T(8,128)(2,1)}, s32[]{:T(128)}) while((s32[]{:T(128)}, bf16[4,2,512,256]{2,3,1,0:T(8,128)(2,1)}, bf16[4,2,512,768]{3,2,1,0:T(8,128)(2,1)}, s32[]{:T(128)}) %tuple.74), condition=%wide.region_11.12_spmd, body=%wide.region_8.11_spmd.sunk | while | flops 558105088 | bytes 46203448 | solution.py:54
  225.3 8.8 %fusion.113 = (f32[2,8,512]{2,1,0:T(8,128)S(1)}, f32[2,8,512,512]{2,3,1,0:T(8,128)}) fusion(bf16[2,512,8,32]{1,3,2,0:T(8,128)(2,1)S(1)} %bitcast.189, bf16[2,512,8,32]{1,3,2,0:T(8,128)(2,1)S(1)} %bitcast.188), kind=kOutput, calls=%fused_computation.109.clone.1 | convolution fusion | flops 281018880 | bytes 17858560 | tf_op jit(solution)/shard_map/while/body/eval_jaxpr/vmap()/sub | solution.py:41
  234.2 7.3 %fusion.114 = bf16[2,8,32,512]{3,2,1,0:T(8,128)(2,1)S(1)} fusion(bf16[2,512,8,32]{1,3,2,0:T(8,128)(2,1)S(1)} %bitcast.185, f32[2,8,512,512]{2,3,1,0:T(8,128)} %get-tuple-element.170, f32[2,8,512]{2,1,0:T(8,128)S(1)} %get-tuple-element.171), kind=kOutput, calls=%fused_computation.20.clone.1 | convolution fusion | flops 277086208 | bytes 17858560 | tf_op jit(solution)/shard_map/while/body/eval_jaxpr/vmap(hqk,khd->qhd)/dot_general | solution.py:43
  244.7 8.8 %fusion.113 = (f32[2,8,512]{2,1,0:T(8,128)S(1)}, f32[2,8,512,512]{2,3,1,0:T(8,128)}) fusion(bf16[2,512,8,32]{1,3,2,0:T(8,128)(2,1)S(1)} %bitcast.189, bf16[2,512,8,32]{1,3,2,0:T(8,128)(2,1)S(1)} %bitcast.188), kind=kOutput, calls=%fused_computation.109.clone.1 | convolution fusion | flops 281018880 | bytes 17858560 | tf_op jit(solution)/shard_map/while/body/eval_jaxpr/vmap()/sub | solution.py:41
  253.6 7.3 %fusion.114 = bf16[2,8,32,512]{3,2,1,0:T(8,128)(2,1)S(1)} fusion(bf16[2,512,8,32]{1,3,2,0:T(8,128)(2,1)S(1)} %bitcast.185, f32[2,8,512,512]{2,3,1,0:T(8,128)} %get-tuple-element.170, f32[2,8,512]{2,1,0:T(8,128)S(1)} %get-tuple-element.171), kind=kOutput, calls=%fused_computation.20.clone.1 | convolution fusion | flops 277086208 | bytes 17858560 | tf_op jit(solution)/shard_map/while/body/eval_jaxpr/vmap(hqk,khd->qhd)/dot_general | solution.py:43
  264.1 8.8 %fusion.113 = (f32[2,8,512]{2,1,0:T(8,128)S(1)}, f32[2,8,512,512]{2,3,1,0:T(8,128)}) fusion(bf16[2,512,8,32]{1,3,2,0:T(8,128)(2,1)S(1)} %bitcast.189, bf16[2,512,8,32]{1,3,2,0:T(8,128)(2,1)S(1)} %bitcast.188), kind=kOutput, calls=%fused_computation.109.clone.1 | convolution fusion | flops 281018880 | bytes 17858560 | tf_op jit(solution)/shard_map/while/body/eval_jaxpr/vmap()/sub | solution.py:41
  272.9 7.3 %fusion.114 = bf16[2,8,32,512]{3,2,1,0:T(8,128)(2,1)S(1)} fusion(bf16[2,512,8,32]{1,3,2,0:T(8,128)(2,1)S(1)} %bitcast.185, f32[2,8,512,512]{2,3,1,0:T(8,128)} %get-tuple-element.170, f32[2,8,512]{2,1,0:T(8,128)S(1)} %get-tuple-element.171), kind=kOutput, calls=%fused_computation.20.clone.1 | convolution fusion | flops 277086208 | bytes 17858560 | tf_op jit(solution)/shard_map/while/body/eval_jaxpr/vmap(hqk,khd->qhd)/dot_general | solution.py:43
  283.5 8.8 %fusion.113 = (f32[2,8,512]{2,1,0:T(8,128)S(1)}, f32[2,8,512,512]{2,3,1,0:T(8,128)}) fusion(bf16[2,512,8,32]{1,3,2,0:T(8,128)(2,1)S(1)} %bitcast.189, bf16[2,512,8,32]{1,3,2,0:T(8,128)(2,1)S(1)} %bitcast.188), kind=kOutput, calls=%fused_computation.109.clone.1 | convolution fusion | flops 281018880 | bytes 17858560 | tf_op jit(solution)/shard_map/while/body/eval_jaxpr/vmap()/sub | solution.py:41
  292.3 7.3 %fusion.114 = bf16[2,8,32,512]{3,2,1,0:T(8,128)(2,1)S(1)} fusion(bf16[2,512,8,32]{1,3,2,0:T(8,128)(2,1)S(1)} %bitcast.185, f32[2,8,512,512]{2,3,1,0:T(8,128)} %get-tuple-element.170, f32[2,8,512]{2,1,0:T(8,128)S(1)} %get-tuple-element.171), kind=kOutput, calls=%fused_computation.20.clone.1 | convolution fusion | flops 277086208 | bytes 17858560 | tf_op jit(solution)/shard_map/while/body/eval_jaxpr/vmap(hqk,khd->qhd)/dot_general | solution.py:43
  300.5 2.8 copy.116
  303.3 2.9 fusion.29
  307.8 27.2 %all_to_all.56 = bf16[2,512,4,256]{3,2,0,1:T(4,128)(2,1)S(1)} all-to-all(bf16[2,512,4,256]{3,2,0,1:T(4,128)(2,1)S(1)} %copy.117), channel_id=1, replica_groups=mesh['gy'=8,'gx'=16] {'gy'}, dimensions={1} | all-to-all | bytes 4194304 | tf_op jit(solution)/shard_map/all_to_all | solution.py:96
  344.3 3.2 collective-permute-done.1
  347.7 7.4 %collective-permute-start.2 = (bf16[2,66,1,256]{3,2,1,0:T(2,128)(2,1)S(1)}, bf16[2,66,1,256]{3,2,1,0:T(2,128)(2,1)S(1)}, u32[]{:S(2)}, u32[]{:S(2)}) collective-permute-start(bf16[2,66,1,256]{3,2,1,0:T(2,128)(2,1)S(1)} %get-tuple-element.99), channel_id=1, source_target_pairs={{0,1},{1,2},{2,3},{3,4},{4,5},{5,6},{6,7},{7,8},{8,9},{9,10},{10,1... | collective-permute-start | bytes 202760 | tf_op jit(solution)/shard_map/ppermute | solution.py:16
  357.1 4.4 %collective-permute-done.3 = bf16[2,66,1,256]{3,2,1,0:T(2,128)(2,1)S(1)} collective-permute-done((bf16[2,66,1,256]{3,2,1,0:T(2,128)(2,1)S(1)}, bf16[2,66,1,256]{3,2,1,0:T(2,128)(2,1)S(1)}, u32[]{:S(2)}, u32[]{:S(2)}) %collective-permute-start.3) | collective-permute-done | bytes 67616 | tf_op jit(solution)/shard_map/ppermute | solution.py:17
  361.5 10.4 %fusion.25 = bf16[2,64,32,256]{3,2,1,0:T(8,128)(2,1)} fusion(bf16[2,64,32,256]{3,2,1,0:T(8,128)(2,1)S(1)} %all_to_all.49, bf16[2,66,32,256]{3,2,1,0:T(8,128)(2,1)S(1)} %constant_dynamic-update-slice_fusion.2, bf16[2,66,1,256]{3,2,1,0:T(2,128)(2,1)S(1)} %collective-permute-done.3, bf16[2,66,1,256]{3,2,1,0:T(2,128)(2,1)S(1)} %collective-permute-done.2, ...), kind=kOutput, calls=%fused_computation.31 | convolution fusion | flops 597688320 | bytes 8930304 | tf_op jit(solution)/shard_map/dot_general | solution.py:113
  (101 shorter events, 70.5 us)
Async XLA Ops:
  0.0 51.8 %copy-start = (bf16[256,768]{1,0:T(8,128)(2,1)S(1)}, bf16[256,768]{1,0:T(8,128)(2,1)}, u32[]{:S(2)}) copy-start(bf16[256,768]{1,0:T(8,128)(2,1)} %param.20) | copy-start | bytes 1179652
  6.0 10.6 %copy-start.9 = (f32[2,256]{1,0:T(2,128)S(1)}, f32[2,256]{1,0:T(2,128)}, u32[]{:S(2)}) copy-start(f32[2,256]{1,0:T(2,128)} %param.19) | copy-start | bytes 6148
  7.5 37.7 %all-to-all-start = ((bf16[2,64,32,256]{3,2,0,1:T(8,128)(2,1)}), bf16[2,64,32,256]{3,2,0,1:T(8,128)(2,1)S(1)}, u32[]{:S(2)}, u32[]{:S(2)}) async-start(bf16[2,64,32,256]{3,2,0,1:T(8,128)(2,1)} %copy.102), calls=%async_computation | async-start | bytes 4194304 | tf_op jit(solution)/shard_map/all_to_all | solution.py:87
  48.3 2.0 copy-start.3
  57.7 77.6 %copy-start.5 = (bf16[256,256]{1,0:T(8,128)(2,1)S(1)}, bf16[256,256]{1,0:T(8,128)(2,1)}, u32[]{:S(2)}) copy-start(bf16[256,256]{1,0:T(8,128)(2,1)} %param.21) | copy-start | bytes 393220
  211.1 4.5 %copy-start.8 = (f32[1,256]{1,0:T(1,128)S(1)}, f32[1,256]{1,0:T(1,128)}, u32[]{:S(2)}) copy-start(f32[1,256]{1,0:T(1,128)} %get-tuple-element.112) | copy-start | bytes 3076
  213.6 2.0 copy-start.2
  213.6 3.4 copy-start.4
  300.5 2.8 copy-start.6
  337.5 19.5 %copy-start.7 = (f32[3,3,256]{2,1,0:T(4,128)S(1)}, f32[3,3,256]{2,1,0:T(4,128)}, u32[]{:S(2)}) copy-start(f32[3,3,256]{2,1,0:T(4,128)} %param.24) | copy-start | bytes 27652
  337.5 23.9 %copy-start.10 = (bf16[256,256]{1,0:T(8,128)(2,1)S(1)}, bf16[256,256]{1,0:T(8,128)(2,1)}, u32[]{:S(2)}) copy-start(bf16[256,256]{1,0:T(8,128)(2,1)} %param.25) | copy-start | bytes 393220
  340.1 4.0 %collective-permute-start = (bf16[2,1,32,256]{3,2,1,0:T(8,128)(2,1)S(1)}, bf16[2,1,32,256]{3,2,1,0:T(8,128)(2,1)S(1)}, u32[]{:S(2)}, u32[]{:S(2)}) collective-permute-start(bf16[2,1,32,256]{3,2,1,0:T(8,128)(2,1)S(1)} %get-tuple-element.102), channel_id=1, source_target_pairs={{0,16},{16,32},{32,48},{48,64},{64,80},{80,96},{96,112},{1,17},{17... | collective-permute-start | bytes 98312 | tf_op jit(solution)/shard_map/ppermute | solution.py:16
  342.8 4.7 %collective-permute-start.1 = (bf16[2,1,32,256]{3,2,1,0:T(8,128)(2,1)S(1)}, bf16[2,1,32,256]{3,2,1,0:T(8,128)(2,1)S(1)}, u32[]{:S(2)}, u32[]{:S(2)}) collective-permute-start(bf16[2,1,32,256]{3,2,1,0:T(8,128)(2,1)S(1)} %get-tuple-element.101), channel_id=1, source_target_pairs={{16,0},{32,16},{48,32},{64,48},{80,64},{96,80},{112,96},{17,1},{33... | collective-permute-start | bytes 98312 | tf_op jit(solution)/shard_map/ppermute | solution.py:17
  347.7 9.4 %collective-permute-start.2 = (bf16[2,66,1,256]{3,2,1,0:T(2,128)(2,1)S(1)}, bf16[2,66,1,256]{3,2,1,0:T(2,128)(2,1)S(1)}, u32[]{:S(2)}, u32[]{:S(2)}) collective-permute-start(bf16[2,66,1,256]{3,2,1,0:T(2,128)(2,1)S(1)} %get-tuple-element.99), channel_id=1, source_target_pairs={{0,1},{1,2},{2,3},{3,4},{4,5},{5,6},{6,7},{7,8},{8,9},{9,10},{10,1... | collective-permute-start | bytes 202760 | tf_op jit(solution)/shard_map/ppermute | solution.py:16
  355.1 6.3 %collective-permute-start.3 = (bf16[2,66,1,256]{3,2,1,0:T(2,128)(2,1)S(1)}, bf16[2,66,1,256]{3,2,1,0:T(2,128)(2,1)S(1)}, u32[]{:S(2)}, u32[]{:S(2)}) collective-permute-start(bf16[2,66,1,256]{3,2,1,0:T(2,128)(2,1)S(1)} %get-tuple-element.100), channel_id=1, source_target_pairs={{1,0},{2,1},{3,2},{4,3},{5,4},{6,5},{7,6},{8,7},{9,8},{10,9},{11,1... | collective-permute-start | bytes 202760 | tf_op jit(solution)/shard_map/ppermute | solution.py:17
  361.5 10.4 %copy-start.1 = (bf16[256,768]{1,0:T(8,128)(2,1)S(1)}, bf16[256,768]{1,0:T(8,128)(2,1)}, u32[]{:S(2)}) copy-start(bf16[256,768]{1,0:T(8,128)(2,1)} %param.20) | copy-start | bytes 1179652
where the time goes:
time: 378 us; the launch traced here: 372 us
  matrix products  157 us (42%)
  blocking collectives  90.9 us (24%)
  local copies, waits for them, and re-layouts  53.7 us (14%)
  waiting for transfers between devices  35.6 us (9%)
  starting transfers between devices  22.4 us (6%)
  other arithmetic  12 us (3%)
    sub x8, matrix products, attend_line(): weights = jnp.exp(scores - row_max)  70.6 us
    dot_general x8, matrix products, attend_line(): jnp.einsum('hqk,khd->qhd', probs, values, preferred_element_type=jnp.floa...  58.5 us
    all_to_all x1, blocking collectives, per_device(): lax.all_to_all(rows_done, 'gx', split_axis=2, concat_axis=1, tiled=True)  33.5 us
    all_to_all x1, blocking collectives, per_device(): lax.all_to_all(tiles, 'gy', split_axis=2, concat_axis=1, tiled=True)  30.1 us
    all_to_all x1, waiting for transfers between devices, per_device(): lax.all_to_all(pillars, 'gx', split_axis=1, concat_axis=2, tiled=True)  28.1 us
    all_to_all x1, blocking collectives, per_device(): lax.all_to_all(col_section, 'gy', split_axis=1, concat_axis=2, tiled=True)  27.2 us
    dynamic_slice x16, local copies, waits for them, and re-layouts, axial(): lax.map(attend_line, packed.reshape(-1, dims_now[2], dims_now[3]), batch_...  17.8 us
    dot_general x1, matrix products, per_device(): jnp.dot(activated, point_weight, preferred_element_type=jnp.float32)  10.4 us
  transfers between devices with their start and end apart: 5, of which 3 were waited for; matrix products, arithmetic and copies ran while one was open for 0% of the time, Pallas kernels for 0%

commit v1 on v0

v1 whole, which is shorter than its diff:
```python
import functools

import jax
import jax.numpy as jnp
from jax import lax
from jax.experimental import pallas as pl
from jax.experimental.pallas import tpu as pltpu
from jax.sharding import PartitionSpec as P

HEADS = 8
BF = jnp.bfloat16
F32 = jnp.float32
LOG2E = 1.4426950408889634
MESH = pl.DeviceIdType.MESH
DEPTH = 48


def dot(a, b):
    return jnp.dot(a, b, preferred_element_type=F32)


def section(x, gain, wqkv_ref, wout_ref):
    length, ch = x.shape
    half_ch = ch // 2
    head_dim = ch // HEADS
    cen = x - jnp.mean(x, -1, keepdims=True)
    var = jnp.mean(cen * cen, -1, keepdims=True)
    normed = (cen * lax.rsqrt(var + 1e-5) * gain).astype(BF)
    q = (dot(normed, wqkv_ref[:, :ch]) * (LOG2E * head_dim ** -0.5)).astype(BF)
    k = dot(normed, wqkv_ref[:, ch : 2 * ch]).astype(BF)
    v = dot(normed, wqkv_ref[:, 2 * ch :]).astype(BF)
    ones = jnp.ones((length, half_ch), BF)
    lane = lax.broadcasted_iota(jnp.int32, (1, ch), 1) // head_dim
    halves = []
    for half in range(2):
        num = den = None
        vals = jnp.concatenate([v[:, half * half_ch : (half + 1) * half_ch], ones], 1)
        for head in range(half * HEADS // 2, (half + 1) * HEADS // 2):
            qm = jnp.where(lane == head, q, BF(0))
            s = lax.dot_general(qm, k, (((1,), (1,)), ((), ())), preferred_element_type=F32)
            e = jnp.exp2(s - jnp.max(s, -1, keepdims=True)).astype(BF)
            r = dot(e, vals)
            if num is None:
                num, den = r[:, :half_ch], r[:, half_ch:]
            else:
                mine = lane[:, half * half_ch : (half + 1) * half_ch] == head
                num = jnp.where(mine, r[:, :half_ch], num)
                den = jnp.where(mine, r[:, half_ch:], den)
        halves.append((num / den).astype(BF))
    return x + dot(jnp.concatenate(halves, 1), wout_ref[...])


class Plan:
    def __init__(self, ny, nx, height, width):
        self.ny, self.nx = ny, nx
        self.height, self.width = height, width
        self.th, self.tw = height // ny, width // nx
        self.rows = 2 * self.th // nx
        self.cols = 2 * self.tw // ny
        self.groups = width // self.cols
        self.per_tile = ny // 2

    def me(self):
        gy, gx = lax.axis_index("gy"), lax.axis_index("gx")
        return gy, gx, lax.rem(gx + gy, 2)

    def owner(self, group, sample):
        gx = group // self.per_tile
        gy = 2 * lax.rem(group, self.per_tile) + lax.rem(sample + gx, 2)
        return (gy, gx)


def row_kernel(pn, feat_ref, emb_ref, g_ref, wqkv_ref, wout_ref, out_ref, x_s, s_s, send_sem, recv_sem, own_sem):
    gy, gx, sample = pn.me()
    ch = emb_ref.shape[1]
    group = gx * pn.per_tile + gy // 2
    row_group = gy * (pn.nx // 2) + gx // 2
    barrier = pltpu.get_barrier_semaphore()

    def greet(t, carry):
        other = pn.owner(lax.rem(group + t, pn.groups), sample)
        pl.semaphore_signal(barrier, inc=1, device_id=other, device_id_type=MESH)
        return carry

    lax.fori_loop(1, pn.groups, greet, 0)

    def pillars(src, carry):
        p = lax.dot_general(feat_ref[src], emb_ref[...], (((0,), (0,)), ((), ())), preferred_element_type=F32)
        x_s[:, pl.ds(pl.multiple_of(src * pn.tw, pn.tw), pn.tw), :] = p.astype(BF).reshape(pn.rows, pn.tw, ch)
        return carry

    lax.fori_loop(0, pn.nx, pillars, 0)
    pl.semaphore_wait(barrier, pn.groups - 1)

    def pair(p, carry):
        done = [
            section(x_s[2 * p + i].astype(F32), g_ref[...], wqkv_ref, wout_ref).reshape(pn.groups, pn.cols, ch)
            for i in range(2)
        ]
        s_s[p] = jnp.concatenate(done, 1).astype(BF)

        def send(t, c):
            to = lax.rem(group + t, pn.groups)
            pltpu.make_async_remote_copy(
                src_ref=s_s.at[p, to],
                dst_ref=out_ref.at[row_group, p],
                send_sem=send_sem,
                recv_sem=recv_sem,
                device_id=pn.owner(to, sample),
                device_id_type=MESH,
            ).start()
            return c

        lax.fori_loop(1, pn.groups, send, 0)
        return carry

    lax.fori_loop(0, pn.rows // 2, pair, 0)
    own = pltpu.make_async_copy(s_s.at[:, group], out_ref.at[row_group], own_sem)
    own.start()
    own.wait()
    arrived = out_ref.at[pl.ds(0, pn.groups - 1)]
    pltpu.make_async_copy(arrived, arrived, send_sem).wait()
    pltpu.make_async_copy(arrived, arrived, recv_sem).wait()


def row_phase(pn, feat, emb, gain, wqkv, wout):
    ch = emb.shape[1]
    vmem = pl.BlockSpec(memory_space=pltpu.VMEM)
    pairs = pn.rows // 2
    return pl.pallas_call(
        functools.partial(row_kernel, pn),
        out_shape=jax.ShapeDtypeStruct((pn.groups, pairs, 2 * pn.cols, ch), BF),
        in_specs=[vmem] * 5,
        out_specs=pl.BlockSpec(memory_space=pl.ANY),
        scratch_shapes=[
            pltpu.VMEM((pn.rows, pn.width, ch), BF),
            pltpu.VMEM((pairs, pn.groups, 2 * pn.cols, ch), BF),
            pltpu.SemaphoreType.DMA,
            pltpu.SemaphoreType.DMA,
            pltpu.SemaphoreType.DMA,
        ],
        compiler_params=pltpu.CompilerParams(
            collective_id=0, has_side_effects=True, vmem_limit_bytes=56 * 2**20
        ),
        name="row_phase",
    )(feat, emb, gain, wqkv, wout)


def col_kernel(
    pn, x_ref, g_ref, wqkv_ref, wout_ref, dk_ref, pw_ref, out_ref, cd_s, o_s, hsend, hrecv, send_sem, recv_sem, own_sem
):
    gy, gx, sample = pn.me()
    group = gx * pn.per_tile + gy // 2
    first = sample * pn.tw + (gy // 2) * pn.cols
    has_left, has_right = group > 0, group < pn.groups - 1
    left = pn.owner(jnp.maximum(group - 1, 0), sample)
    right = pn.owner(jnp.minimum(group + 1, pn.groups - 1), sample)
    last = pn.cols - 1
    barrier = pltpu.get_barrier_semaphore()

    def greet(t, carry):
        pl.semaphore_signal(
            barrier, inc=1, device_id=(lax.rem(gy + t, pn.ny), gx), device_id_type=MESH
        )
        return carry

    lax.fori_loop(1, pn.ny, greet, 0)

    @pl.when(has_left)
    def _():
        pl.semaphore_signal(barrier, inc=1, device_id=left, device_id_type=MESH)

    @pl.when(has_right)
    def _():
        pl.semaphore_signal(barrier, inc=1, device_id=right, device_id_type=MESH)

    zeros = jnp.zeros(cd_s.shape[1:], BF)

    @pl.when(jnp.logical_not(has_left))
    def _():
        cd_s[0] = zeros

    @pl.when(jnp.logical_not(has_right))
    def _():
        cd_s[pn.cols + 1] = zeros

    to_left = pltpu.make_async_remote_copy(
        src_ref=cd_s.at[1],
        dst_ref=cd_s.at[pn.cols + 1],
        send_sem=hsend.at[0],
        recv_sem=hrecv.at[0],
        device_id=left,
        device_id_type=MESH,
    )
    to_right = pltpu.make_async_remote_copy(
        src_ref=cd_s.at[pn.cols],
        dst_ref=cd_s.at[0],
        send_sem=hsend.at[1],
        recv_sem=hrecv.at[1],
        device_id=right,
        device_id_type=MESH,
    )
    row = lax.broadcasted_iota(jnp.int32, (pn.height, 1), 0)

    def conv(c):
        near = [cd_s[c + i].astype(F32) for i in range(3)]
        taps = [sum(near[e] * dk_ref[a, e, :][None] for e in range(3)) for a in range(3)]
        above = jnp.where(row == 0, 0.0, pltpu.roll(taps[0], 1, 0))
        below = jnp.where(row == pn.height - 1, 0.0, pltpu.roll(taps[2], pn.height - 1, 0))
        depth = above + taps[1] + below
        act = (depth / (1.0 + jnp.exp(-depth))).astype(BF)
        o_s[c] = (near[1] + dot(act, pw_ref[...])).astype(BF)

        def send(t, carry):
            to = lax.rem(gy + t, pn.ny)
            pltpu.make_async_remote_copy(
                src_ref=o_s.at[c, pl.ds(pl.multiple_of(to * pn.th, pn.th), pn.th)],
                dst_ref=out_ref.at[first + c],
                send_sem=send_sem,
                recv_sem=recv_sem,
                device_id=(to, gx),
                device_id_type=MESH,
            ).start()
            return carry

        lax.fori_loop(1, pn.ny, send, 0)

    def line(t, carry):
        c = jnp.where(t == 0, 0, jnp.where(t == 1, last, t - 1))
        cd_s[c + 1] = section(x_ref[c].astype(F32), g_ref[...], wqkv_ref, wout_ref).astype(BF)

        @pl.when(jnp.logical_and(t == 0, has_left))
        def _():
            to_left.start()

        @pl.when(jnp.logical_and(t == 1, has_right))
        def _():
            to_right.start()

        @pl.when(t >= 2)
        def _():
            @pl.when(jnp.logical_and(t == 2, has_left))
            def _():
                to_right.wait_recv()

            conv(t - 2)

        return carry

    pl.semaphore_wait(barrier, pn.ny - 1 + has_left.astype(jnp.int32) + has_right.astype(jnp.int32))
    lax.fori_loop(0, pn.cols, line, 0)

    def tail(c, carry):
        @pl.when(jnp.logical_and(c == last, has_right))
        def _():
            to_left.wait_recv()

        conv(c)
        return carry

    lax.fori_loop(pn.cols - 2, pn.cols, tail, 0)

    own = pltpu.make_async_copy(
        o_s.at[:, pl.ds(pl.multiple_of(gy * pn.th, pn.th), pn.th)], out_ref.at[pl.ds(first, pn.cols)], own_sem
    )
    own.start()
    own.wait()

    @pl.when(has_left)
    def _():
        to_left.wait_send()

    @pl.when(has_right)
    def _():
        to_right.wait_send()

    arrived = out_ref.at[pl.ds(0, (pn.ny - 1) * pn.cols)]
    pltpu.make_async_copy(arrived, arrived, send_sem).wait()
    pltpu.make_async_copy(arrived, arrived, recv_sem).wait()


def col_phase(pn, cols, gain, wqkv, wout, dk, pw):
    ch = cols.shape[-1]
    vmem = pl.BlockSpec(memory_space=pltpu.VMEM)
    return pl.pallas_call(
        functools.partial(col_kernel, pn),
        out_shape=jax.ShapeDtypeStruct((2 * pn.tw, pn.th, ch), BF),
        in_specs=[vmem] * 6,
        out_specs=pl.BlockSpec(memory_space=pl.ANY),
        scratch_shapes=[
            pltpu.VMEM((pn.cols + 2, pn.height, ch), BF),
            pltpu.VMEM((pn.cols, pn.height, ch), BF),
            pltpu.SemaphoreType.DMA((2,)),
            pltpu.SemaphoreType.DMA((2,)),
            pltpu.SemaphoreType.DMA,
            pltpu.SemaphoreType.DMA,
            pltpu.SemaphoreType.DMA,
        ],
        compiler_params=pltpu.CompilerParams(
            collective_id=1, has_side_effects=True, vmem_limit_bytes=56 * 2**20
        ),
        name="col_phase",
    )(cols, gain, wqkv, wout, dk, pw)


def split3(x):
    a = lax.reduce_precision(x, 8, 7)
    b = lax.reduce_precision(x - a, 8, 7)
    c = lax.reduce_precision(x - a - b, 8, 7)
    return a, b, c


def per_device(
    occupancy,
    counts,
    level_embed,
    count_weight,
    norm_gains,
    row_qkv,
    row_out,
    col_qkv,
    col_out,
    depth_kernel,
    point_weight,
):
    ny, nx = lax.axis_size("gy"), lax.axis_size("gx")
    th, tw = counts.shape[1:]
    levels, ch = level_embed.shape
    pn = Plan(ny, nx, th * ny, tw * nx)
    gy = lax.axis_index("gy")

    l1, l2, l3 = split3(jnp.log1p(counts.astype(F32)))
    w1, w2, w3 = split3(count_weight)
    zero = jnp.zeros_like(l1)
    feat = jnp.concatenate(
        [occupancy.astype(BF), jnp.stack([l1, l1, l1, l2, l2, l3] + [zero] * (DEPTH - levels - 6), 1).astype(BF)], 1
    )
    emb = jnp.concatenate(
        [
            level_embed,
            jnp.stack([w1, w2, w3, w1, w2, w1]).astype(BF),
            jnp.zeros((DEPTH - levels - 6, ch), BF),
        ]
    )
    feat = jnp.where(lax.rem(gy, 2) == 1, feat[::-1], feat)
    feat = feat.reshape(2, DEPTH, nx // 2, pn.rows, tw).transpose(2, 0, 1, 3, 4).reshape(nx, DEPTH, pn.rows * tw)
    feat = lax.all_to_all(feat, "gx", split_axis=0, concat_axis=0, tiled=True)

    got = row_phase(pn, feat, emb, norm_gains[:1], row_qkv, row_out)
    cols = got.reshape(pn.height, pn.cols, ch).transpose(1, 0, 2)
    out = col_phase(pn, cols, norm_gains[1:], col_qkv, col_out, depth_kernel, point_weight)
    return out.reshape(2, tw, th, ch).transpose(0, 2, 1, 3)


def solution(mesh):
    in_specs = (P(None, None, "gy", "gx"), P(None, "gy", "gx")) + (P(),) * 9
    out_specs = P(None, "gy", "gx", None)
    return jax.shard_map(
        per_device, mesh=mesh, in_specs=in_specs, out_specs=out_specs, check_vma=False
    )
```

time: 378 us -> 134 us (0.35); the launches traced: 372 us -> 133 us
  matrix products: 157 us -> 0 us
  Pallas kernels: 0 us -> 97.6 us
  blocking collectives: 90.9 us -> 0 us
  local copies, waits for them, and re-layouts: 53.7 us -> 14.9 us
  waiting for transfers between devices: 35.6 us -> 7.89 us
  starting transfers between devices: 22.4 us -> 9.13 us
  other arithmetic: 12 us -> 3.3 us
    pallas_call x0 -> x2, Pallas kernels: none -> 97.6 us  [the longest x1 51.5 us: col_phase(): pl.pallas_call(functools.partial(col_kernel, pn), out_shape=jax.ShapeDtyp...]
    all_to_all x3 -> x0, blocking collectives: 90.9 us -> none  [the longest x1 33.5 us: per_device(): lax.all_to_all(rows_done, 'gx', split_axis=2, concat_axis=1, tiled=True)]
    dot_general x14 -> x0, matrix products: 86.2 us -> none  [the longest x8 58.5 us: attend_line(): jnp.einsum('hqk,khd->qhd', probs, values, preferred_element_type=jnp.floa...]
    sub x8 -> x0, matrix products: 70.6 us -> none  [attend_line(): weights = jnp.exp(scores - row_max)]
    all_to_all x1, waiting for transfers between devices: 28.1 us -> 7.89 us  [per_device(): feat = lax.all_to_all(feat, 'gx', split_axis=0, concat_axis=0, tiled=True)]
    dynamic_slice x16 -> x0, local copies, waits for them, and re-layouts: 17.8 us -> none  [axial(): lax.map(attend_line, packed.reshape(-1, dims_now[2], dims_now[3]), batch_...]
    ppermute x4 -> x0, starting transfers between devices: 13.3 us -> none  [the longest x2 10.1 us: extended(): before = lax.ppermute(last, axis, up)]
    convert_element_type x6 -> x0, local copies, waits for them, and re-layouts: 9.55 us -> none  [the longest x2 3.24 us: axial(): return (source.astype(jnp.float32) + jnp.dot(attended, w_out, preferred_e...]
  transfers between devices with their start and end apart: 5 -> 1, of which waited for: 3 -> 1; matrix products, arithmetic and copies ran while one was open for 0% -> 1% of each run, Pallas kernels for 0% -> 0%
where the time goes in v1:
time: 134 us; the launch traced here: 133 us
  Pallas kernels  97.6 us (73%)
  local copies, waits for them, and re-layouts  14.9 us (11%)
  starting transfers between devices  9.13 us (7%)
  waiting for transfers between devices  7.89 us (6%)
  other arithmetic  3.3 us (2%)
    pallas_call x1, Pallas kernels, col_phase(): pl.pallas_call(functools.partial(col_kernel, pn), out_shape=jax.ShapeDtyp...  51.5 us
    pallas_call x1, Pallas kernels, row_phase(): pl.pallas_call(functools.partial(row_kernel, pn), out_shape=jax.ShapeDtyp...  46.1 us
    all_to_all x1, starting transfers between devices, per_device(): feat = lax.all_to_all(feat, 'gx', split_axis=0, concat_axis=0, tiled=True)  9.13 us
    all_to_all x1, waiting for transfers between devices, per_device(): feat = lax.all_to_all(feat, 'gx', split_axis=0, concat_axis=0, tiled=True)  7.89 us
    reshape x1, local copies, waits for them, and re-layouts, per_device(): return out.reshape(2, tw, th, ch).transpose(0, 2, 1, 3)  4.09 us
    reshape x1, local copies, waits for them, and re-layouts, per_device(): cols = got.reshape(pn.height, pn.cols, ch).transpose(1, 0, 2)  3.34 us
    unnamed x7, other arithmetic  3.14 us
  transfers between devices with their start and end apart: 1, of which 1 were waited for; matrix products, arithmetic and copies ran while one was open for 1% of the time, Pallas kernels for 0%

profile of v1, /device:TPU:1, one launch (start us, length us, event | category | flops | bytes accessed | tf_op | source)
XLA Modules:
  0.0 132.9 jit_solution(1244384048200186126)
XLA Ops:
  0.0 0.0 copy-start.1
  0.0 1.5 %convert_dynamic-update-slice_fusion = bf16[2,48,64,32]{2,3,1,0:T(8,128)(2,1)S(1)} fusion(s32[2,40,64,32]{2,3,1,0:T(8,128)} %param.11), kind=kLoop, calls=%fused_computation.3 | loop fusion | flops 163839 | bytes 1310720
  1.5 0.8 constant_dynamic-update-slice_fusion.6
  2.2 0.8 constant_dynamic-update-slice_fusion.5
  3.0 0.0 copy-done.1
  3.2 0.2 reverse_select_fusion
  3.3 2.0 %copy.43 = bf16[2,48,64,32]{1,3,2,0:T(8,128)(2,1)S(1)} copy(bf16[2,48,64,32]{2,3,1,0:T(8,128)(2,1)S(1)} %reverse_select_fusion) | data formatting | bytes 786432 | tf_op jit(solution)/shard_map/jit(_where)/select_n | solution.py:345
  5.3 0.0 copy-start.4
  5.3 0.0 copy-start.2
  5.3 0.0 copy-start.3
  5.3 1.0 copy.44
  6.4 1.8 %reshape.13 = bf16[16,48,256]{2,1,0:T(8,128)(2,1)} reshape(bf16[8,2,48,8,32]{4,3,2,1,0:T(8,128)(2,1)S(1)} %copy.44) | data formatting | bytes 786432 | tf_op jit(solution)/shard_map/reshape | solution.py:346
  8.2 9.1 %all-to-all-start = ((bf16[16,48,256]{2,1,0:T(8,128)(2,1)}), bf16[16,48,256]{2,1,0:T(8,128)(2,1)S(1)}, u32[]{:S(2)}, u32[]{:S(2)}) async-start(bf16[16,48,256]{2,1,0:T(8,128)(2,1)} %reshape.13), calls=%async_computation | async-start | bytes 786432 | tf_op jit(solution)/shard_map/all_to_all | solution.py:347
  17.4 0.0 copy-done.4
  17.4 0.0 copy-done.2
  17.4 1.2 concatenate.9.emb_ref
  18.6 0.0 copy-done.3
  18.6 0.6 fusion.7
  19.2 7.9 %all-to-all-done.feat_ref = bf16[16,48,256]{2,1,0:T(8,128)(2,1)S(1)} async-done(((bf16[16,48,256]{2,1,0:T(8,128)(2,1)}), bf16[16,48,256]{2,1,0:T(8,128)(2,1)S(1)}, u32[]{:S(2)}, u32[]{:S(2)}) %all-to-all-start) | async-done | bytes 393248 | tf_op jit(solution)/shard_map/all_to_all | solution.py:347
  27.1 0.0 copy-start
  27.1 0.7 copy-done
  27.9 46.1 %row_phase.1 = bf16[64,4,16,256]{3,2,1,0:T(8,128)(2,1)} custom-call(bf16[16,48,256]{2,1,0:T(8,128)(2,1)} %copy-done, bf16[48,256]{1,0:T(8,128)(2,1)} %concatenate.9.emb_ref, f32[1,256]{1,0:T(1,128)} %get-tuple-element.6.g_ref, bf16[256,768]{1,0:T(8,128)(2,1)} %wqkv_ref.2, bf16[256,256]{1,0:T(8,128)(2,1)} %wout_ref.2), custom_call_target="tpu_custom_call" | custom-call | tf_op jit(solution)/shard_map/row_phase/pallas_call | solution.py:130
  74.0 3.3 %copy.50 = bf16[512,8,256]{2,0,1:T(8,128)(2,1)} copy(bf16[512,8,256]{2,1,0:T(8,128)(2,1)} %bitcast.33) | data formatting | bytes 4194304 | tf_op jit(solution)/shard_map/reshape | solution.py:350
  77.4 51.5 %col_phase.1 = bf16[64,64,256]{2,1,0:T(8,128)(2,1)} custom-call(bf16[8,512,256]{2,1,0:T(8,128)(2,1)} %bitcast.34, f32[1,256]{1,0:T(1,128)} %get-tuple-element.5.g_ref, bf16[256,768]{1,0:T(8,128)(2,1)} %wqkv_ref.3, bf16[256,256]{1,0:T(8,128)(2,1)} %wout_ref.3, f32[3,3,256]{2,1,0:T(4,128)} %dk_ref.1, bf16[256,256]{1,0:T(8,128)(2,1)} %pw_ref.1), custom_call_target="tpu_custom_call" | custom-call | tf_op jit(solution)/shard_map/col_phase/pallas_call | solution.py:285
  128.8 4.1 %copy.49 = bf16[2,32,64,256]{3,1,2,0:T(8,128)(2,1)} copy(bf16[2,32,64,256]{3,2,1,0:T(8,128)(2,1)} %bitcast.35) | data formatting | bytes 4194304 | tf_op jit(solution)/shard_map/reshape | solution.py:352
  (10 shorter events, 0.1 us)
Async XLA Ops:
  0.0 3.0 %copy-start.1 = (s32[2,64,32]{1,2,0:T(8,128)S(1)}, s32[2,64,32]{1,2,0:T(8,128)}, u32[]{:S(2)}) copy-start(s32[2,64,32]{1,2,0:T(8,128)} %param.12) | copy-start | bytes 49156
  5.3 12.1 %copy-start.4 = (f32[256]{0:T(256)S(1)}, f32[256]{0:T(256)}, u32[]{:S(2)}) copy-start(f32[256]{0:T(256)} %param.14) | copy-start | bytes 3076
  5.3 12.1 %copy-start.2 = (bf16[40,256]{1,0:T(8,128)(2,1)S(1)}, bf16[40,256]{1,0:T(8,128)(2,1)}, u32[]{:S(2)}) copy-start(bf16[40,256]{1,0:T(8,128)(2,1)} %param.13) | copy-start | bytes 61444
  5.3 13.3 %copy-start.3 = (f32[2,256]{1,0:T(2,128)S(1)}, f32[2,256]{1,0:T(2,128)}, u32[]{:S(2)}) copy-start(f32[2,256]{1,0:T(2,128)} %param.15) | copy-start | bytes 6148
  8.2 18.9 %all-to-all-start = ((bf16[16,48,256]{2,1,0:T(8,128)(2,1)}), bf16[16,48,256]{2,1,0:T(8,128)(2,1)S(1)}, u32[]{:S(2)}, u32[]{:S(2)}) async-start(bf16[16,48,256]{2,1,0:T(8,128)(2,1)} %reshape.13), calls=%async_computation | async-start | bytes 786432 | tf_op jit(solution)/shard_map/all_to_all | solution.py:347
  27.1 0.7 copy-start

commit v2 on v0

v2 whole, which is shorter than its diff:
```python
import functools

import jax
import jax.numpy as jnp
from jax import lax
from jax.experimental import pallas as pl
from jax.experimental.pallas import tpu as pltpu
from jax.sharding import PartitionSpec as P

HEADS = 8
BF = jnp.bfloat16
F32 = jnp.float32
LOG2E = 1.4426950408889634
MESH = pl.DeviceIdType.MESH
DEPTH = 48
LANES = 128


def dot(a, b):
    return jnp.dot(a, b, preferred_element_type=F32)


def section(x, gain, wqkv_ref, wout_ref):
    length, ch = x.shape
    half_ch = ch // 2
    head_dim = ch // HEADS
    cen = x - jnp.mean(x, -1, keepdims=True)
    var = jnp.mean(cen * cen, -1, keepdims=True)
    normed = (cen * lax.rsqrt(var + 1e-5) * gain).astype(BF)
    q = (dot(normed, wqkv_ref[:, :ch]) * (LOG2E * head_dim ** -0.5)).astype(BF)
    k = dot(normed, wqkv_ref[:, ch : 2 * ch]).astype(BF)
    v = dot(normed, wqkv_ref[:, 2 * ch :]).astype(BF)
    ones = jnp.ones((length, half_ch), BF)
    lane = lax.broadcasted_iota(jnp.int32, (1, ch), 1) // head_dim
    halves = []
    for half in range(2):
        num = den = None
        vals = jnp.concatenate([v[:, half * half_ch : (half + 1) * half_ch], ones], 1)
        for head in range(half * HEADS // 2, (half + 1) * HEADS // 2):
            qm = jnp.where(lane == head, q, BF(0))
            s = lax.dot_general(qm, k, (((1,), (1,)), ((), ())), preferred_element_type=F32)
            e = jnp.exp2(s - jnp.max(s, -1, keepdims=True)).astype(BF)
            r = dot(e, vals)
            if num is None:
                num, den = r[:, :half_ch], r[:, half_ch:]
            else:
                mine = lane[:, half * half_ch : (half + 1) * half_ch] == head
                num = jnp.where(mine, r[:, :half_ch], num)
                den = jnp.where(mine, r[:, half_ch:], den)
        halves.append((num / den).astype(BF))
    return x + dot(jnp.concatenate(halves, 1), wout_ref[...])


def split3(x):
    a = x.astype(BF).astype(F32)
    b = (x - a).astype(BF).astype(F32)
    return a, b, x - a - b


class Plan:
    def __init__(self, ny, nx, height, width):
        self.ny, self.nx = ny, nx
        self.n = ny * nx
        self.height, self.width = height, width
        self.th, self.tw = height // ny, width // nx
        self.rows = height // self.n
        self.cols = width // self.n
        self.per_group = LANES // self.tw
        self.pairs = DEPTH // self.per_group // 2

    def snake(self, q):
        return jnp.where(q < self.ny // 2, q, 3 * self.ny // 2 - 1 - q)

    def owner(self, group):
        m = lax.rem(group, 2 * self.ny)
        return (self.snake(m // 2), 2 * (group // (2 * self.ny)) + lax.rem(m, 2))


def kernel(
    pn,
    occ_ref, cnt_ref, emb_ref, cw_ref, g_ref, rqkv_ref, rout_ref, cqkv_ref, cout_ref, dk_ref, pw_ref,
    out_ref,
    snd_s, got_s, lhs_s, ee_s, x_s, s_s, r_s, xr_s, cd_s, o_s,
    occ_sems, row_send, row_recv, hsend, hrecv, out_sems,
):
    ny, nx, n = pn.ny, pn.nx, pn.n
    th, tw, rows, cols = pn.th, pn.tw, pn.rows, pn.cols
    ch = emb_ref.shape[1]
    levels = emb_ref.shape[0]
    gy, gx = lax.axis_index("gy"), lax.axis_index("gx")
    core = lax.rem(gx, 2)
    m = 2 * pn.snake(gy) + core
    group = (gx // 2) * (2 * ny) + m
    row_group = gy * nx + gx
    tile_x = 2 * (gx // 2) + m // ny
    first = lax.rem(m, ny) * cols
    has_left, has_right = group > 0, group < n - 1
    left = pn.owner(jnp.maximum(group - 1, 0))
    right = pn.owner(jnp.minimum(group + 1, n - 1))
    barrier = pltpu.get_barrier_semaphore()

    def greet(t, carry):
        pl.semaphore_signal(
            barrier, inc=1, device_id=pn.owner(lax.rem(group + t, n)), device_id_type=MESH
        )
        return carry

    lax.fori_loop(1, n, greet, 0)

    def lined_up(b):
        logs = split3(jnp.log1p(cnt_ref[b].astype(F32)))
        terms = [logs[i] for i in (0, 0, 0, 1, 1, 2)]
        return jnp.concatenate(
            [occ_ref[b].astype(F32).reshape(levels * tw, th)]
            + terms
            + [jnp.zeros(((DEPTH - levels - len(terms)) * tw, th), F32)],
            0,
        )

    turned = jnp.concatenate([lined_up(0), lined_up(1)], 1).T
    t0 = turned[:th].reshape(th // 8, 8, DEPTH * tw)
    t1 = turned[th:].reshape(th // 8, 8, DEPTH * tw)
    sub = lax.broadcasted_iota(jnp.int32, (1, 8, 1), 1) < 4
    both = (jnp.where(sub, t0, pltpu.roll(t1, 4, 1)), jnp.where(sub, pltpu.roll(t0, 4, 1), t1))
    for t in range(th // 8):
        for i in range(2):
            for p in range(pn.pairs):
                part = both[i][t][:, 2 * p * LANES : 2 * (p + 1) * LANES]
                snd_s[2 * t + i, p] = jnp.concatenate([part[:, :LANES], part[:, LANES:]], 0).astype(BF)

    pl.semaphore_wait(barrier, n - 1)

    def send_occ(t, carry):
        to = lax.rem(gx + t, nx)
        pltpu.make_async_remote_copy(
            src_ref=snd_s.at[to],
            dst_ref=got_s.at[gx],
            send_sem=occ_sems.at[0],
            recv_sem=occ_sems.at[1],
            device_id=(gy, to),
            device_id_type=MESH,
        ).start()
        return carry

    lax.fori_loop(1, nx, send_occ, 0)
    got_s[gx] = snd_s[gx]

    w1, w2, w3 = split3(cw_ref[...])
    table = [emb_ref[i : i + 1, :].astype(F32) for i in range(levels)] + [w1, w2, w3, w1, w2, w1]
    zero = jnp.zeros((8, ch), F32)
    for i in range(pn.per_group):
        for j in range(LANES // 8):
            at = j * pn.per_group + i
            r0 = i * LANES + j * 8
            ee_s[r0 : r0 + 8, :] = jnp.broadcast_to(table[at], (8, ch)) if at < len(table) else zero

    for s in range(2):
        arrived = got_s.at[pl.ds(0, nx - 1)]
        pltpu.make_async_copy(arrived, arrived, occ_sems.at[s]).wait()

    def unpack(src, carry):
        rows_in = got_s[src].reshape(pn.pairs * 16, LANES).astype(F32)
        pad = jnp.zeros((LANES - pn.pairs * 16, LANES), F32)
        back = jnp.concatenate([rows_in, pad], 0).T.astype(BF)
        for i in range(pn.per_group):
            lhs_s[pl.ds(pl.multiple_of(src * tw, tw), tw), i * LANES : (i + 1) * LANES] = back[
                i * tw : (i + 1) * tw
            ]
        return carry

    lax.fori_loop(0, nx, unpack, 0)
    which = lax.broadcasted_iota(jnp.int32, (pn.per_group * LANES, 1), 0) % 8

    def pillars(i, carry):
        x_s[i] = dot(lhs_s[...], jnp.where(which == i, ee_s[...], 0.0).astype(BF)).astype(BF)
        return carry

    lax.fori_loop(0, 2 * rows, pillars, 0)

    def row_sample(b, carry):
        y = [
            section(x_s[b * rows + i].astype(F32), g_ref[0:1, :], rqkv_ref, rout_ref).reshape(n // 2, 8, ch)
            for i in range(4)
        ]
        even = [jnp.where(sub, y[i], pltpu.roll(y[i + 1], 4, 1)) for i in (0, 2)]
        odd = [jnp.where(sub, pltpu.roll(y[i], 4, 1), y[i + 1]) for i in (0, 2)]
        s_s[b, :, 0] = jnp.concatenate(even, 1).astype(BF)
        s_s[b, :, 1] = jnp.concatenate(odd, 1).astype(BF)

        def send(t, c):
            to = lax.rem(group + t, n)
            pltpu.make_async_remote_copy(
                src_ref=s_s.at[b, to // 2, lax.rem(to, 2)],
                dst_ref=r_s.at[b, row_group],
                send_sem=row_send.at[b],
                recv_sem=row_recv.at[b],
                device_id=pn.owner(to),
                device_id_type=MESH,
            ).start()
            return c

        lax.fori_loop(1, n, send, 0)
        r_s[b, row_group] = s_s[b, group // 2, lax.rem(group, 2)]
        return carry

    lax.fori_loop(0, 2, row_sample, 0)

    edge = jnp.zeros(cd_s.shape[2:], BF)
    for b in range(2):

        @pl.when(jnp.logical_not(has_left))
        def _():
            cd_s[b, 0] = edge

        @pl.when(jnp.logical_not(has_right))
        def _():
            cd_s[b, cols + 1] = edge

    row = lax.broadcasted_iota(jnp.int32, (pn.height, 1), 0)

    def halo(b, side):
        return pltpu.make_async_remote_copy(
            src_ref=cd_s.at[b, cols if side else 1],
            dst_ref=cd_s.at[b, 0 if side else cols + 1],
            send_sem=hsend.at[b, side],
            recv_sem=hrecv.at[b, side],
            device_id=right if side else left,
            device_id_type=MESH,
        )

    def col_sample(b, carry):
        blocks = r_s.at[b, pl.ds(0, n - 1)]
        pltpu.make_async_copy(blocks, blocks, row_recv.at[b]).wait()
        for i in range(ch // LANES):
            xr_s[i] = r_s[b, :, :, i * LANES : (i + 1) * LANES].astype(F32).reshape(pn.height * cols, LANES)

        def two(u, c):
            for i in range(2):
                at = u if i == 0 else cols - 1 - u
                x = jnp.concatenate(
                    [xr_s[j, pl.ds(at, pn.height, stride=cols), :] for j in range(ch // LANES)], 1
                )
                cd_s[b, at + 1] = section(x, g_ref[1:2, :], cqkv_ref, cout_ref).astype(BF)

            @pl.when(jnp.logical_and(u == 0, has_left))
            def _():
                halo(b, 0).start()

            @pl.when(jnp.logical_and(u == 0, has_right))
            def _():
                halo(b, 1).start()

            return c

        lax.fori_loop(0, cols // 2, two, 0)

        @pl.when(has_left)
        def _():
            halo(b, 1).wait_recv()

        @pl.when(has_right)
        def _():
            halo(b, 0).wait_recv()

        def conv(i, c):
            near = [cd_s[b, i + e].astype(F32) for e in range(3)]
            taps = [sum(near[e] * dk_ref[a, e, :][None] for e in range(3)) for a in range(3)]
            above = jnp.where(row == 0, 0.0, pltpu.roll(taps[0], 1, 0))
            below = jnp.where(row == pn.height - 1, 0.0, pltpu.roll(taps[2], pn.height - 1, 0))
            depth = above + taps[1] + below
            act = (depth / (1.0 + jnp.exp(-depth))).astype(BF)
            o_s[b, i] = (near[1] + dot(act, pw_ref[...])).astype(BF)

            def send(t, cc):
                to = lax.rem(gy + t, ny)
                src = o_s.at[b, i, pl.ds(pl.multiple_of(to * th, th), th)]
                dst = out_ref.at[b * tw + first + i]
                away = jnp.logical_or(t > 0, tile_x != gx)

                @pl.when(away)
                def _():
                    pltpu.make_async_remote_copy(
                        src_ref=src,
                        dst_ref=dst,
                        send_sem=out_sems.at[0],
                        recv_sem=out_sems.at[1],
                        device_id=(to, tile_x),
                        device_id_type=MESH,
                    ).start()

                @pl.when(jnp.logical_not(away))
                def _():
                    pltpu.make_async_copy(src, dst, out_sems.at[2]).start()

                return cc

            lax.fori_loop(0, ny, send, 0)
            return c

        lax.fori_loop(0, cols, conv, 0)
        return carry

    lax.fori_loop(0, 2, col_sample, 0)

    for b in range(2):
        blocks = r_s.at[b, pl.ds(0, n - 1)]
        pltpu.make_async_copy(blocks, blocks, row_send.at[b]).wait()

        @pl.when(has_left)
        def _():
            halo(b, 0).wait_send()

        @pl.when(has_right)
        def _():
            halo(b, 1).wait_send()

    local = tile_x == gx

    def wait_out(count, s):
        part = out_ref.at[pl.ds(0, count)]
        pltpu.make_async_copy(part, part, out_sems.at[s]).wait()

    @pl.when(local)
    def _():
        wait_out(2 * cols * (ny - 1), 0)
        wait_out(2 * cols * (ny - 1), 1)
        wait_out(2 * cols, 2)

    @pl.when(jnp.logical_not(local))
    def _():
        wait_out(2 * cols * ny, 0)
        wait_out(2 * cols * ny, 1)


def per_device(
    occupancy,
    counts,
    level_embed,
    count_weight,
    norm_gains,
    row_qkv,
    row_out,
    col_qkv,
    col_out,
    depth_kernel,
    point_weight,
):
    ny, nx = lax.axis_size("gy"), lax.axis_size("gx")
    th, tw = counts.shape[1:]
    ch = level_embed.shape[1]
    pn = Plan(ny, nx, th * ny, tw * nx)
    vmem = pl.BlockSpec(memory_space=pltpu.VMEM)
    out = pl.pallas_call(
        functools.partial(kernel, pn),
        out_shape=jax.ShapeDtypeStruct((2 * tw, th, ch), BF),
        in_specs=[vmem] * 11,
        out_specs=pl.BlockSpec(memory_space=pl.ANY),
        scratch_shapes=[
            pltpu.VMEM((nx, pn.pairs, 16, LANES), BF),
            pltpu.VMEM((nx, pn.pairs, 16, LANES), BF),
            pltpu.VMEM((pn.width, pn.per_group * LANES), BF),
            pltpu.VMEM((pn.per_group * LANES, ch), F32),
            pltpu.VMEM((2 * pn.rows, pn.width, ch), BF),
            pltpu.VMEM((2, pn.n // 2, 2, 16, ch), BF),
            pltpu.VMEM((2, pn.n, 16, ch), BF),
            pltpu.VMEM((ch // LANES, pn.height * pn.cols, LANES), F32),
            pltpu.VMEM((2, pn.cols + 2, pn.height, ch), BF),
            pltpu.VMEM((2, pn.cols, pn.height, ch), BF),
            pltpu.SemaphoreType.DMA((2,)),
            pltpu.SemaphoreType.DMA((2,)),
            pltpu.SemaphoreType.DMA((2,)),
            pltpu.SemaphoreType.DMA((2, 2)),
            pltpu.SemaphoreType.DMA((2, 2)),
            pltpu.SemaphoreType.DMA((3,)),
        ],
        compiler_params=pltpu.CompilerParams(
            collective_id=0, has_side_effects=True, vmem_limit_bytes=60 * 2**20
        ),
        name="block",
    )(
        occupancy.transpose(0, 1, 3, 2),
        counts.transpose(0, 2, 1),
        level_embed,
        count_weight[None],
        norm_gains,
        row_qkv,
        row_out,
        col_qkv,
        col_out,
        depth_kernel,
        point_weight,
    )
    return out.reshape(2, tw, th, ch).transpose(0, 2, 1, 3)


def solution(mesh):
    in_specs = (P(None, None, "gy", "gx"), P(None, "gy", "gx")) + (P(),) * 9
    out_specs = P(None, "gy", "gx", None)
    return jax.shard_map(
        per_device, mesh=mesh, in_specs=in_specs, out_specs=out_specs, check_vma=False
    )
```

time: 378 us -> 107 us (0.28); the launches traced: 372 us -> 107 us
  matrix products: 157 us -> 0 us
  Pallas kernels: 0 us -> 102 us
  blocking collectives: 90.9 us -> 0 us
  local copies, waits for them, and re-layouts: 53.7 us -> 4.09 us
  waiting for transfers between devices: 35.6 us -> 0 us
  starting transfers between devices: 22.4 us -> 0 us
  other arithmetic: 12 us -> 0 us
    pallas_call x0 -> x1, Pallas kernels: none -> 102 us  [per_device(): pl.pallas_call(functools.partial(kernel, pn), out_shape=jax.ShapeDtypeStr...]
    all_to_all x3 -> x0, blocking collectives: 90.9 us -> none  [the longest x1 33.5 us: per_device(): lax.all_to_all(rows_done, 'gx', split_axis=2, concat_axis=1, tiled=True)]
    dot_general x14 -> x0, matrix products: 86.2 us -> none  [the longest x8 58.5 us: attend_line(): jnp.einsum('hqk,khd->qhd', probs, values, preferred_element_type=jnp.floa...]
    sub x8 -> x0, matrix products: 70.6 us -> none  [attend_line(): weights = jnp.exp(scores - row_max)]
    all_to_all x1 -> x0, waiting for transfers between devices: 28.1 us -> none  [per_device(): lax.all_to_all(pillars, 'gx', split_axis=1, concat_axis=2, tiled=True)]
    dynamic_slice x16 -> x0, local copies, waits for them, and re-layouts: 17.8 us -> none  [axial(): lax.map(attend_line, packed.reshape(-1, dims_now[2], dims_now[3]), batch_...]
    ppermute x4 -> x0, starting transfers between devices: 13.3 us -> none  [the longest x2 10.1 us: extended(): before = lax.ppermute(last, axis, up)]
    convert_element_type x6 -> x0, local copies, waits for them, and re-layouts: 9.55 us -> none  [the longest x2 3.24 us: axial(): return (source.astype(jnp.float32) + jnp.dot(attended, w_out, preferred_e...]
  transfers between devices with their start and end apart: 5 -> 0, of which waited for: 3 -> 0; matrix products, arithmetic and copies ran while one was open for 0% -> 0% of each run, Pallas kernels for 0% -> 0%
where the time goes in v2:
time: 107 us
  Pallas kernels  102 us (95%)
  local copies, waits for them, and re-layouts  4.09 us (4%)
    pallas_call x1, Pallas kernels, per_device(): pl.pallas_call(functools.partial(kernel, pn), out_shape=jax.ShapeDtypeStr...  102 us
    reshape x1, local copies, waits for them, and re-layouts, per_device(): return out.reshape(2, tw, th, ch).transpose(0, 2, 1, 3)  4.09 us

profile of v2, /device:TPU:1, one launch (start us, length us, event | category | flops | bytes accessed | tf_op | source)
XLA Modules:
  0.0 106.5 jit_solution(1572420679915274049)
XLA Ops:
  0.0 102.4 %block.1 = bf16[64,64,256]{2,1,0:T(8,128)(2,1)} custom-call(s32[2,40,32,64]{3,2,1,0:T(8,128)} %bitcast.8, s32[2,32,64]{2,1,0:T(8,128)} %bitcast.9, bf16[40,256]{1,0:T(8,128)(2,1)} %emb_ref.1, f32[1,256]{1,0:T(1,128)} %bitcast.10, f32[2,256]{1,0:T(2,128)} %g_ref.1, bf16[256,768]{1,0:T(8,128)(2,1)} %rqkv_ref.1, bf16[256,256]{1,0:T(8,128)(2,1)} %rout_ref.1, ...), custom_call_target="tpu_custom_call" | custom-call | tf_op jit(solution)/shard_map/block/pallas_call | solution.py:353
  102.4 4.1 %copy.14 = bf16[2,32,64,256]{3,1,2,0:T(8,128)(2,1)} copy(bf16[2,32,64,256]{3,2,1,0:T(8,128)(2,1)} %bitcast.7) | data formatting | bytes 4194304 | tf_op jit(solution)/shard_map/reshape | solution.py:393

commit v3 on v2

--- a/solution.py
+++ b/solution.py
@@ -81,7 +81,7 @@
     occ_ref, cnt_ref, emb_ref, cw_ref, g_ref, rqkv_ref, rout_ref, cqkv_ref, cout_ref, dk_ref, pw_ref,
     out_ref,
     snd_s, got_s, lhs_s, ee_s, x_s, s_s, r_s, xr_s, cd_s, o_s,
-    occ_sems, row_send, row_recv, hsend, hrecv, out_sems,
+    all_in, occ_sems, row_send, row_recv, hsend, hrecv, out_sems,
 ):
     ny, nx, n = pn.ny, pn.nx, pn.n
     th, tw, rows, cols = pn.th, pn.tw, pn.rows, pn.cols
@@ -99,13 +99,16 @@
     right = pn.owner(jnp.minimum(group + 1, n - 1))
     barrier = pltpu.get_barrier_semaphore()
 
-    def greet(t, carry):
-        pl.semaphore_signal(
-            barrier, inc=1, device_id=pn.owner(lax.rem(group + t, n)), device_id_type=MESH
-        )
-        return carry
-
-    lax.fori_loop(1, n, greet, 0)
+    def greet(sem, along_x):
+        def one(t, carry):
+            other = (gy, lax.rem(gx + t, nx)) if along_x else (lax.rem(gy + t, ny), gx)
+            pl.semaphore_signal(sem, inc=1, device_id=other, device_id_type=MESH)
+            return carry
+
+        lax.fori_loop(1, nx if along_x else ny, one, 0)
+
+    greet(barrier, True)
+    greet(barrier, False)
 
     def lined_up(b):
         logs = split3(jnp.log1p(cnt_ref[b].astype(F32)))
@@ -128,7 +131,7 @@
                 part = both[i][t][:, 2 * p * LANES : 2 * (p + 1) * LANES]
                 snd_s[2 * t + i, p] = jnp.concatenate([part[:, :LANES], part[:, LANES:]], 0).astype(BF)
 
-    pl.semaphore_wait(barrier, n - 1)
+    pl.semaphore_wait(barrier, nx - 1 + ny - 1)
 
     def send_occ(t, carry):
         to = lax.rem(gx + t, nx)
@@ -144,6 +147,7 @@
 
     lax.fori_loop(1, nx, send_occ, 0)
     got_s[gx] = snd_s[gx]
+    greet(all_in, False)
 
     w1, w2, w3 = split3(cw_ref[...])
     table = [emb_ref[i : i + 1, :].astype(F32) for i in range(levels)] + [w1, w2, w3, w1, w2, w1]
@@ -168,14 +172,15 @@
             ]
         return carry
 
-    lax.fori_loop(0, nx, unpack, 0)
+    lax.fori_loop(0, nx, unpack, 0, unroll=16)
     which = lax.broadcasted_iota(jnp.int32, (pn.per_group * LANES, 1), 0) % 8
 
     def pillars(i, carry):
         x_s[i] = dot(lhs_s[...], jnp.where(which == i, ee_s[...], 0.0).astype(BF)).astype(BF)
         return carry
 
-    lax.fori_loop(0, 2 * rows, pillars, 0)
+    lax.fori_loop(0, 2 * rows, pillars, 0, unroll=2)
+    pl.semaphore_wait(all_in, ny - 1)
 
     def row_sample(b, carry):
         y = [
@@ -187,8 +192,8 @@
         s_s[b, :, 0] = jnp.concatenate(even, 1).astype(BF)
         s_s[b, :, 1] = jnp.concatenate(odd, 1).astype(BF)
 
-        def send(t, c):
-            to = lax.rem(group + t, n)
+        def send(t):
+            to = lax.rem(group + 37 * t, n)
             pltpu.make_async_remote_copy(
                 src_ref=s_s.at[b, to // 2, lax.rem(to, 2)],
                 dst_ref=r_s.at[b, row_group],
@@ -197,9 +202,15 @@
                 device_id=pn.owner(to),
                 device_id_type=MESH,
             ).start()
+
+        def send_some(t, c):
+            for i in range(7):
+                send(t * 7 + i + 1)
             return c
 
-        lax.fori_loop(1, n, send, 0)
+        lax.fori_loop(0, (n - 1) // 7, send_some, 0)
+        for t in range((n - 1) // 7 * 7 + 1, n):
+            send(t)
         r_s[b, row_group] = s_s[b, group // 2, lax.rem(group, 2)]
         return carry
 
@@ -234,33 +245,11 @@
         for i in range(ch // LANES):
             xr_s[i] = r_s[b, :, :, i * LANES : (i + 1) * LANES].astype(F32).reshape(pn.height * cols, LANES)
 
-        def two(u, c):
-            for i in range(2):
-                at = u if i == 0 else cols - 1 - u
-                x = jnp.concatenate(
-                    [xr_s[j, pl.ds(at, pn.height, stride=cols), :] for j in range(ch // LANES)], 1
-                )
-                cd_s[b, at + 1] = section(x, g_ref[1:2, :], cqkv_ref, cout_ref).astype(BF)
-
-            @pl.when(jnp.logical_and(u == 0, has_left))
-            def _():
-                halo(b, 0).start()
-
-            @pl.when(jnp.logical_and(u == 0, has_right))
-            def _():
-                halo(b, 1).start()
-
-            return c
-
-        lax.fori_loop(0, cols // 2, two, 0)
-
-        @pl.when(has_left)
-        def _():
-            halo(b, 1).wait_recv()
-
-        @pl.when(has_right)
-        def _():
-            halo(b, 0).wait_recv()
+        def line(at):
+            x = jnp.concatenate(
+                [xr_s[j, pl.ds(at, pn.height, stride=cols), :] for j in range(ch // LANES)], 1
+            )
+            cd_s[b, at + 1] = section(x, g_ref[1:2, :], cqkv_ref, cout_ref).astype(BF)
 
         def conv(i, c):
             near = [cd_s[b, i + e].astype(F32) for e in range(3)]
@@ -272,7 +261,7 @@
             o_s[b, i] = (near[1] + dot(act, pw_ref[...])).astype(BF)
 
             def send(t, cc):
-                to = lax.rem(gy + t, ny)
+                to = lax.rem(gy + 3 * t, ny)
                 src = o_s.at[b, i, pl.ds(pl.multiple_of(to * th, th), th)]
                 dst = out_ref.at[b * tw + first + i]
                 away = jnp.logical_or(t > 0, tile_x != gx)
@@ -297,7 +286,36 @@
             lax.fori_loop(0, ny, send, 0)
             return c
 
-        lax.fori_loop(0, cols, conv, 0)
+        line(0)
+        line(cols - 1)
+
+        @pl.when(has_left)
+        def _():
+            halo(b, 0).start()
+
+        @pl.when(has_right)
+        def _():
+            halo(b, 1).start()
+
+        line(1)
+
+        @pl.when(has_left)
+        def _():
+            halo(b, 1).wait_recv()
+
+        @pl.when(has_right)
+        def _():
+            halo(b, 0).wait_recv()
+
+        def last_two(i, c):
+            @pl.when(i == 1)
+            def _():
+                line(2)
+
+            conv(i, 0)
+            return c
+
+        lax.fori_loop(0, cols, last_two, 0)
         return carry
 
     lax.fori_loop(0, 2, col_sample, 0)
@@ -366,6 +384,7 @@
             pltpu.VMEM((ch // LANES, pn.height * pn.cols, LANES), F32),
             pltpu.VMEM((2, pn.cols + 2, pn.height, ch), BF),
             pltpu.VMEM((2, pn.cols, pn.height, ch), BF),
+            pltpu.SemaphoreType.REGULAR,
             pltpu.SemaphoreType.DMA((2,)),
             pltpu.SemaphoreType.DMA((2,)),
             pltpu.SemaphoreType.DMA((2,)),

time: 107 us -> 101 us (0.944)
  Pallas kernels: 102 us -> 96.5 us
    pallas_call x1, Pallas kernels: 102 us -> 96.5 us  [per_device(): pl.pallas_call(functools.partial(kernel, pn), out_shape=jax.ShapeDtypeStr...]
where the time goes in v3:
time: 101 us
  Pallas kernels  96.5 us (96%)
  local copies, waits for them, and re-layouts  4.09 us (4%)
    pallas_call x1, Pallas kernels, per_device(): pl.pallas_call(functools.partial(kernel, pn), out_shape=jax.ShapeDtypeStr...  96.5 us
    reshape x1, local copies, waits for them, and re-layouts, per_device(): return out.reshape(2, tw, th, ch).transpose(0, 2, 1, 3)  4.09 us

profile of v3, /device:TPU:1, one launch (start us, length us, event | category | flops | bytes accessed | tf_op | source)
XLA Modules:
  0.0 100.6 jit_solution(2795524603570964496)
XLA Ops:
  0.0 96.5 %block.1 = bf16[64,64,256]{2,1,0:T(8,128)(2,1)} custom-call(s32[2,40,32,64]{3,2,1,0:T(8,128)} %bitcast.8, s32[2,32,64]{2,1,0:T(8,128)} %bitcast.9, bf16[40,256]{1,0:T(8,128)(2,1)} %emb_ref.1, f32[1,256]{1,0:T(1,128)} %bitcast.10, f32[2,256]{1,0:T(2,128)} %g_ref.1, bf16[256,768]{1,0:T(8,128)(2,1)} %rqkv_ref.1, bf16[256,256]{1,0:T(8,128)(2,1)} %rout_ref.1, ...), custom_call_target="tpu_custom_call" | custom-call | tf_op jit(solution)/shard_map/block/pallas_call | solution.py:371
  96.5 4.1 %copy.14 = bf16[2,32,64,256]{3,1,2,0:T(8,128)(2,1)} copy(bf16[2,32,64,256]{3,2,1,0:T(8,128)(2,1)} %bitcast.7) | data formatting | bytes 4194304 | tf_op jit(solution)/shard_map/reshape | solution.py:412

commit v4 on v3

--- a/solution.py
+++ b/solution.py
@@ -193,13 +193,15 @@
         s_s[b, :, 1] = jnp.concatenate(odd, 1).astype(BF)
 
         def send(t):
-            to = lax.rem(group + 37 * t, n)
+            u = lax.rem(37 * t + gy * nx + gx, n)
+            to_y, to_x = lax.div(u, nx), lax.rem(u, nx)
+            q = pn.snake(to_y)
             pltpu.make_async_remote_copy(
-                src_ref=s_s.at[b, to // 2, lax.rem(to, 2)],
+                src_ref=s_s.at[b, lax.div(to_x, 2) * ny + q, lax.rem(to_x, 2)],
                 dst_ref=r_s.at[b, row_group],
                 send_sem=row_send.at[b],
                 recv_sem=row_recv.at[b],
-                device_id=pn.owner(to),
+                device_id=(to_y, to_x),
                 device_id_type=MESH,
             ).start()
 
@@ -287,35 +289,35 @@
             return c
 
         line(0)
-        line(cols - 1)
 
         @pl.when(has_left)
         def _():
             halo(b, 0).start()
 
-        @pl.when(has_right)
-        def _():
-            halo(b, 1).start()
-
         line(1)
-
-        @pl.when(has_left)
-        def _():
-            halo(b, 1).wait_recv()
-
-        @pl.when(has_right)
-        def _():
-            halo(b, 0).wait_recv()
-
-        def last_two(i, c):
+        line(2)
+
+        def last_lines(i, c):
             @pl.when(i == 1)
             def _():
-                line(2)
-
-            conv(i, 0)
+                line(3)
+
+                @pl.when(has_right)
+                def _():
+                    halo(b, 1).start()
+
+            @pl.when(jnp.logical_and(i == 2, has_right))
+            def _():
+                halo(b, 0).wait_recv()
+
+            @pl.when(jnp.logical_and(i == 3, has_left))
+            def _():
+                halo(b, 1).wait_recv()
+
+            conv(lax.rem(i + 1, cols), 0)
             return c
 
-        lax.fori_loop(0, cols, last_two, 0)
+        lax.fori_loop(0, cols, last_lines, 0)
         return carry
 
     lax.fori_loop(0, 2, col_sample, 0)
@@ -348,6 +350,47 @@
     def _():
         wait_out(2 * cols * ny, 0)
         wait_out(2 * cols * ny, 1)
+
+
+def turn_kernel(parts, x_ref, o_ref, x_s, o_s, in_sems, out_sems):
+    samples, _, th, _ = x_ref.shape
+    step = th // parts
+
+    def bring(b, i):
+        rows = pl.ds(i * step, step)
+        return pltpu.make_async_copy(x_ref.at[b, :, rows], x_s.at[b, :, rows], in_sems.at[b, i])
+
+    def leave(b, i):
+        rows = pl.ds(i * step, step)
+        return pltpu.make_async_copy(o_s.at[b, rows], o_ref.at[b, rows], out_sems.at[b, i])
+
+    order = [(b, i) for b in range(samples) for i in range(parts)]
+    for at in order:
+        bring(*at).start()
+    for b, i in order:
+        bring(b, i).wait()
+        o_s[b, i * step : (i + 1) * step] = jnp.swapaxes(x_s[b, :, i * step : (i + 1) * step], 0, 1)
+        leave(b, i).start()
+    for at in order:
+        leave(*at).wait()
+
+
+def turn(x, parts):
+    samples, tw, th, ch = x.shape
+    return pl.pallas_call(
+        functools.partial(turn_kernel, parts),
+        in_specs=[pl.BlockSpec(memory_space=pl.ANY)],
+        out_specs=pl.BlockSpec(memory_space=pl.ANY),
+        out_shape=jax.ShapeDtypeStruct((samples, th, tw, ch), x.dtype),
+        scratch_shapes=[
+            pltpu.VMEM(x.shape, x.dtype),
+            pltpu.VMEM((samples, th, tw, ch), x.dtype),
+            pltpu.SemaphoreType.DMA((samples, parts)),
+            pltpu.SemaphoreType.DMA((samples, parts)),
+        ],
+        compiler_params=pltpu.CompilerParams(vmem_limit_bytes=60 * 2**20),
+        name="turn",
+    )(x)
 
 
 def per_device(
@@ -409,7 +452,7 @@
         depth_kernel,
         point_weight,
     )
-    return out.reshape(2, tw, th, ch).transpose(0, 2, 1, 3)
+    return turn(out.reshape(2, tw, th, ch), 2)
 
 
 def solution(mesh):

time: 101 us -> 98.5 us (0.975); the launches traced: 101 us -> 96.9 us
  local copies, waits for them, and re-layouts: 4.09 us -> 0 us
    reshape x1 -> x0, local copies, waits for them, and re-layouts: 4.09 us -> none  [per_device(): return out.reshape(2, tw, th, ch).transpose(0, 2, 1, 3)]
    pallas_call x0 -> x1, Pallas kernels: none -> 2.55 us  [turn(): pl.pallas_call(functools.partial(turn_kernel, parts), in_specs=[pl.BlockS...]
    pallas_call x1, Pallas kernels: 96.5 us -> 94.2 us  [per_device(): pl.pallas_call(functools.partial(kernel, pn), out_shape=jax.ShapeDtypeStr...]
where the time goes in v4:
time: 98.5 us; the launch traced here: 96.9 us
  Pallas kernels  96.7 us (98%)
    pallas_call x1, Pallas kernels, per_device(): pl.pallas_call(functools.partial(kernel, pn), out_shape=jax.ShapeDtypeStr...  94.2 us
    pallas_call x1, Pallas kernels, turn(): pl.pallas_call(functools.partial(turn_kernel, parts), in_specs=[pl.BlockS...  2.55 us

profile of v4, /device:TPU:1, one launch (start us, length us, event | category | flops | bytes accessed | tf_op | source)
XLA Modules:
  0.0 96.9 jit_solution(6635054723724580234)
XLA Ops:
  0.0 94.2 %block.1 = bf16[64,64,256]{2,1,0:T(8,128)(2,1)} custom-call(s32[2,40,32,64]{3,2,1,0:T(8,128)} %bitcast.5, s32[2,32,64]{2,1,0:T(8,128)} %bitcast.6, bf16[40,256]{1,0:T(8,128)(2,1)} %emb_ref.1, f32[1,256]{1,0:T(1,128)} %bitcast.7, f32[2,256]{1,0:T(2,128)} %g_ref.1, bf16[256,768]{1,0:T(8,128)(2,1)} %rqkv_ref.1, bf16[256,256]{1,0:T(8,128)(2,1)} %rout_ref.1, ...), custom_call_target="tpu_custom_call" | custom-call | tf_op jit(solution)/shard_map/block/pallas_call | solution.py:414
  94.2 2.6 %turn.1 = bf16[2,64,32,256]{3,2,1,0:T(8,128)(2,1)} custom-call(bf16[2,32,64,256]{3,2,1,0:T(8,128)(2,1)} %bitcast.4), custom_call_target="tpu_custom_call" | custom-call | tf_op jit(solution)/shard_map/turn/pallas_call | solution.py:380

commit v5 on v4

--- a/solution.py
+++ b/solution.py
@@ -32,22 +32,35 @@
     v = dot(normed, wqkv_ref[:, 2 * ch :]).astype(BF)
     ones = jnp.ones((length, half_ch), BF)
     lane = lax.broadcasted_iota(jnp.int32, (1, ch), 1) // head_dim
-    halves = []
-    for half in range(2):
-        num = den = None
-        vals = jnp.concatenate([v[:, half * half_ch : (half + 1) * half_ch], ones], 1)
-        for head in range(half * HEADS // 2, (half + 1) * HEADS // 2):
-            qm = jnp.where(lane == head, q, BF(0))
-            s = lax.dot_general(qm, k, (((1,), (1,)), ((), ())), preferred_element_type=F32)
-            e = jnp.exp2(s - jnp.max(s, -1, keepdims=True)).astype(BF)
-            r = dot(e, vals)
-            if num is None:
-                num, den = r[:, :half_ch], r[:, half_ch:]
-            else:
-                mine = lane[:, half * half_ch : (half + 1) * half_ch] == head
-                num = jnp.where(mine, r[:, :half_ch], num)
-                den = jnp.where(mine, r[:, half_ch:], den)
-        halves.append((num / den).astype(BF))
+    vals = [jnp.concatenate([v[:, i * half_ch : (i + 1) * half_ch], ones], 1) for i in range(2)]
+
+    def scores(head):
+        qm = jnp.where(lane == head, q, BF(0))
+        return lax.dot_general(qm, k, (((1,), (1,)), ((), ())), preferred_element_type=F32)
+
+    sums = [None, None]
+
+    def attend(head, e):
+        half = head // (HEADS // 2)
+        r = dot(e, vals[half])
+        parts = (r[:, :half_ch], r[:, half_ch:])
+        if sums[half] is None:
+            sums[half] = parts
+        else:
+            mine = lane[:, half * half_ch : (half + 1) * half_ch] == head
+            sums[half] = tuple(jnp.where(mine, a, b) for a, b in zip(parts, sums[half]))
+
+    s = scores(0)
+    waiting = None
+    for head in range(HEADS):
+        e = jnp.exp2(s - jnp.max(s, -1, keepdims=True)).astype(BF)
+        if head + 1 < HEADS:
+            s = scores(head + 1)
+        if waiting is not None:
+            attend(*waiting)
+        waiting = (head, e)
+    attend(*waiting)
+    halves = [(num * pl.reciprocal(den)).astype(BF) for num, den in sums]
     return x + dot(jnp.concatenate(halves, 1), wout_ref[...])
 
 
@@ -179,10 +192,10 @@
         x_s[i] = dot(lhs_s[...], jnp.where(which == i, ee_s[...], 0.0).astype(BF)).astype(BF)
         return carry
 
-    lax.fori_loop(0, 2 * rows, pillars, 0, unroll=2)
     pl.semaphore_wait(all_in, ny - 1)
 
     def row_sample(b, carry):
+        lax.fori_loop(b * rows, (b + 1) * rows, pillars, 0)
         y = [
             section(x_s[b * rows + i].astype(F32), g_ref[0:1, :], rqkv_ref, rout_ref).reshape(n // 2, 8, ch)
             for i in range(4)
@@ -258,8 +271,8 @@
             taps = [sum(near[e] * dk_ref[a, e, :][None] for e in range(3)) for a in range(3)]
             above = jnp.where(row == 0, 0.0, pltpu.roll(taps[0], 1, 0))
             below = jnp.where(row == pn.height - 1, 0.0, pltpu.roll(taps[2], pn.height - 1, 0))
-            depth = above + taps[1] + below
-            act = (depth / (1.0 + jnp.exp(-depth))).astype(BF)
+            half = 0.5 * (above + taps[1] + below)
+            act = (half * jnp.tanh(half) + half).astype(BF)
             o_s[b, i] = (near[1] + dot(act, pw_ref[...])).astype(BF)
 
             def send(t, cc):

time: 98.5 us -> 97.4 us (0.989)
  no operation moved by 1% of the time
where the time goes in v5:
time: 97.4 us; the launch traced here: 96.5 us
  Pallas kernels  96.4 us (99%)
    pallas_call x1, Pallas kernels, per_device(): pl.pallas_call(functools.partial(kernel, pn), out_shape=jax.ShapeDtypeStr...  93.8 us
    pallas_call x1, Pallas kernels, turn(): pl.pallas_call(functools.partial(turn_kernel, parts), in_specs=[pl.BlockS...  2.55 us

profile of v5, /device:TPU:1, one launch (start us, length us, event | category | flops | bytes accessed | tf_op | source)
XLA Modules:
  0.0 96.5 jit_solution(2081747297300985974)
XLA Ops:
  0.0 93.8 %block.1 = bf16[64,64,256]{2,1,0:T(8,128)(2,1)} custom-call(s32[2,40,32,64]{3,2,1,0:T(8,128)} %bitcast.5, s32[2,32,64]{2,1,0:T(8,128)} %bitcast.6, bf16[40,256]{1,0:T(8,128)(2,1)} %emb_ref.1, f32[1,256]{1,0:T(1,128)} %bitcast.7, f32[2,256]{1,0:T(2,128)} %g_ref.1, bf16[256,768]{1,0:T(8,128)(2,1)} %rqkv_ref.1, bf16[256,256]{1,0:T(8,128)(2,1)} %rout_ref.1, ...), custom_call_target="tpu_custom_call" | custom-call | tf_op jit(solution)/shard_map/block/pallas_call | solution.py:427
  93.8 2.6 %turn.1 = bf16[2,64,32,256]{3,2,1,0:T(8,128)(2,1)} custom-call(bf16[2,32,64,256]{3,2,1,0:T(8,128)(2,1)} %bitcast.4), custom_call_target="tpu_custom_call" | custom-call | tf_op jit(solution)/shard_map/turn/pallas_call | solution.py:393

commit v6 on v5

--- a/solution.py
+++ b/solution.py
@@ -158,7 +158,7 @@
         ).start()
         return carry
 
-    lax.fori_loop(1, nx, send_occ, 0)
+    lax.fori_loop(1, nx, send_occ, 0, unroll=5)
     got_s[gx] = snd_s[gx]
     greet(all_in, False)
 
@@ -465,7 +465,7 @@
         depth_kernel,
         point_weight,
     )
-    return turn(out.reshape(2, tw, th, ch), 2)
+    return turn(out.reshape(2, tw, th, ch), 4)
 
 
 def solution(mesh):

time: 97.4 us -> 97.2 us (level)
  no operation moved by 1% of the time
where the time goes in v6:
time: 97.2 us; the launch traced here: 96.5 us
  Pallas kernels  96.3 us (99%)
    pallas_call x1, Pallas kernels, per_device(): pl.pallas_call(functools.partial(kernel, pn), out_shape=jax.ShapeDtypeStr...  93.8 us
    pallas_call x1, Pallas kernels, turn(): pl.pallas_call(functools.partial(turn_kernel, parts), in_specs=[pl.BlockS...  2.46 us

profile of v6, /device:TPU:1, one launch (start us, length us, event | category | flops | bytes accessed | tf_op | source)
XLA Modules:
  0.0 96.5 jit_solution(10523447056204552582)
XLA Ops:
  0.0 93.8 %block.1 = bf16[64,64,256]{2,1,0:T(8,128)(2,1)} custom-call(s32[2,40,32,64]{3,2,1,0:T(8,128)} %bitcast.5, s32[2,32,64]{2,1,0:T(8,128)} %bitcast.6, bf16[40,256]{1,0:T(8,128)(2,1)} %emb_ref.1, f32[1,256]{1,0:T(1,128)} %bitcast.7, f32[2,256]{1,0:T(2,128)} %g_ref.1, bf16[256,768]{1,0:T(8,128)(2,1)} %rqkv_ref.1, bf16[256,256]{1,0:T(8,128)(2,1)} %rout_ref.1, ...), custom_call_target="tpu_custom_call" | custom-call | tf_op jit(solution)/shard_map/block/pallas_call | solution.py:427
  93.8 2.5 %turn.1 = bf16[2,64,32,256]{3,2,1,0:T(8,128)(2,1)} custom-call(bf16[2,32,64,256]{3,2,1,0:T(8,128)(2,1)} %bitcast.4), custom_call_target="tpu_custom_call" | custom-call | tf_op jit(solution)/shard_map/turn/pallas_call | solution.py:393
